TPU v7x, 32 devices: a whole 2x2x4 slice. The times are simulated.
32 devices in a mesh: seq: 16 (over z, y, x), tp: 2 (over core).
Axes of the slice: x: 2, y: 2, z: 4, core: 2. Of those that a mesh axis runs over, the one named last changes fastest.
Arguments:
- patches: bfloat16 [1664, 16384], P('tp', 'seq'), may hold values from -400 to 400
- ln_gain: bfloat16 [1664], P('tp'), may hold values from 0.099609375 to 1.8984375
- ln_bias: bfloat16 [1664], P('tp'), may hold values from -3 to 3
- merge_weight: bfloat16 [4, 1664, 1664], P(None, 'tp', 'seq'), may hold values from -0.078125 to 0.078125
- merge_bias: bfloat16 [1664], P('tp'), may hold values from -3 to 3
- targets: int32 [4096], P('seq'), may hold values from 0 to 6143, as said below
- text_embed: bfloat16 [1664, 6144], P('tp', 'seq'), may hold values from -6 to 6
Outputs:
- prompt_embeds: bfloat16 [1664, 6144], P('tp', 'seq')
Inputs may be any that keep to these rules, and one draw needn't show every extreme that they name: `targets`: Distinct. The merged rows of one index of seq go to the positions of 8 indices of seq (position p belongs to index p // 384); at most 40 of them to one index, and exactly 40 to some index, from every index.
All inputs are finite; a program needn't handle non-finite values.
Results may differ from a plain program's by a relative error of at most 0.015.
Values may be sent and summed in bfloat16 or wider, within the bound.
A program may use at most 64 MiB of HBM per device.

v0:
```python
import jax
import jax.numpy as jnp
from jax import lax
from jax.sharding import PartitionSpec as P

D = 1664
GROUP = 4


def shards(patches, ln_gain, ln_bias, merge_weight, merge_bias, targets, text_embed):
    values = patches.astype(jnp.float32)
    feature_total = lax.psum(jnp.sum(values, axis=0), "tp")
    row_mean = feature_total / D
    centered = values - row_mean[None, :]
    square_total = lax.psum(jnp.sum(centered * centered, axis=0), "tp")
    row_var = square_total / D
    scaled = (
        centered * lax.rsqrt(row_var + 1e-06)[None, :] * ln_gain.astype(jnp.float32)[:, None]
        + ln_bias.astype(jnp.float32)[:, None]
    )
    normed = scaled.astype(jnp.bfloat16)
    feat_width = normed.shape[0]
    merged_rows = normed.shape[1] // GROUP
    grouped = normed.reshape(feat_width, merged_rows, GROUP)
    partial_terms = jnp.einsum(
        "fmk,kfc->cm",
        grouped,
        lax.all_gather(merge_weight, "seq", axis=2, tiled=True),
        preferred_element_type=jnp.float32,
    )
    summed = lax.psum_scatter(
        partial_terms.astype(jnp.bfloat16), "tp", scatter_dimension=0, tiled=True
    ).astype(jnp.float32)
    merged = (summed + merge_bias.astype(jnp.float32)[:, None]).astype(jnp.bfloat16)
    seq_count = lax.axis_size("seq")
    prompt_rows = text_embed.shape[1]
    capacity = 5 * merged_rows // (2 * seq_count)
    target_dev = targets // prompt_rows
    local_pos = targets % prompt_rows
    one_hot = (target_dev[:, None] == jnp.arange(seq_count, dtype=jnp.int32)[None, :]).astype(
        jnp.int32
    )
    order_in = jnp.sum((jnp.cumsum(one_hot, axis=0) - 1) * one_hot, axis=1)
    slot_index = target_dev * capacity + order_in
    send_rows = (
        jnp.zeros((feat_width, seq_count * capacity), jnp.bfloat16).at[:, slot_index].set(merged)
    )
    send_pos = (
        jnp.full((seq_count * capacity,), prompt_rows, jnp.int32).at[slot_index].set(local_pos)
    )
    got_rows, got_pos = (
        lax.all_to_all(
            send_rows.reshape(feat_width, seq_count, capacity),
            "seq",
            split_axis=1,
            concat_axis=1,
            tiled=True,
        ),
        lax.all_to_all(
            send_pos.reshape(1, seq_count, capacity), "seq", split_axis=1, concat_axis=1, tiled=True
        ),
    )
    return text_embed.at[:, got_pos.reshape(-1)].set(got_rows.reshape(feat_width, -1), mode="drop")


def solution(mesh):
    in_specs = (
        P("tp", "seq"),
        P("tp"),
        P("tp"),
        P(None, "tp", "seq"),
        P("tp"),
        P("seq"),
        P("tp", "seq"),
    )
    out_specs = P("tp", "seq")
    return jax.shard_map(shards, mesh=mesh, in_specs=in_specs, out_specs=out_specs, check_vma=False)
```

profile of v0, /device:TPU:0, one launch (start us, length us, event | category | flops | bytes accessed | tf_op | source)
XLA Modules:
  0.0 226.9 jit_solution(15767506945839548845)
XLA Ops:
  6.5 0.0 copy-start
  6.5 0.0 all-gather.2.cloned.1.call-start
  6.5 0.7 all-gather.2.cloned.1.call-update
  7.3 0.0 reduce-scatter.4.cloned.1.call-start
  7.3 0.7 convert_element_type.34
  8.0 0.7 convert_element_type.35
  8.7 1.7 convert_reduce_fusion
  10.4 2.6 %psum.14 = f32[1024]{0:T(1024)S(1)} all-reduce(f32[1024]{0:T(1024)S(1)} %convert_reduce_fusion), channel_id=1, replica_groups=mesh['seq'=16,'tp'=2] {'tp'}, use_global_device_ids=true, to_apply=%region_5.6 | all-reduce | flops 1024 | bytes 8192 | tf_op jit(solution)/shard_map/psum | solution.py:12
  13.0 0.0 copy-done
  13.0 0.5 fusion.2
  13.5 2.5 %psum.15 = f32[1024]{0:T(1024)S(1)} all-reduce(f32[1024]{0:T(1024)S(1)} %fusion.2), channel_id=1, replica_groups=mesh['seq'=16,'tp'=2] {'tp'}, use_global_device_ids=true, to_apply=%region_7.8 | all-reduce | flops 1024 | bytes 8192 | tf_op jit(solution)/shard_map/psum | solution.py:15
  16.0 0.7 fusion.5
  16.6 1.7 copy.17
  18.3 1.6 reshape.69
  19.9 138.8 %all-gather.2.cloned.1.call-done = bf16[4,832,1664]{1,2,0:T(8,128)(2,1)} async-done(((bf16[4,832,104]{1,2,0:T(8,128)(2,1)}), bf16[4,832,1664]{1,2,0:T(8,128)(2,1)}) %all-gather.2.cloned.1.call-update) | async-done | bytes 11075600 | tf_op jit(solution)/shard_map/all_gather | solution.py:28
  158.7 8.5 %fusion.7 = bf16[1664,256]{0,1:T(8,128)(2,1)S(1)} fusion(bf16[4,832,1664]{1,2,0:T(8,128)(2,1)} %all-gather.2.cloned.1.call-done, bf16[832,256,4]{0,2,1:T(4,128)(2,1)} %reshape.69), kind=kOutput, calls=%fused_computation.13 | convolution fusion | flops 2835775488 | bytes 13631488 | tf_op jit(solution)/shard_map/fmk,kfc->cm/dot_general | solution.py:25
  167.2 0.0 copy-start.3
  167.2 0.0 copy-start.2
  167.2 1.3 copy.21
  168.5 0.0 reduce-scatter.4.cloned.1.call-update
  168.5 0.0 copy-done.3
  168.5 0.6 reduce-window.6
  169.1 0.2 slice_reduce_fusion
  169.4 0.1 fusion.15
  169.5 1.4 scatter_custom_fusion
  170.9 0.7 reshape.67
  171.6 3.8 %all-to-all-start = ((s32[1,16,40]{2,0,1:T(1,128)}), s32[1,16,40]{2,0,1:T(1,128)S(1)}, u32[]{:S(2)}, u32[]{:S(2)}) async-start(s32[1,16,40]{2,0,1:T(1,128)} %reshape.67), calls=%async_computation | async-start | bytes 16384 | tf_op jit(solution)/shard_map/all_to_all | solution.py:59
  175.4 0.0 copy-done.2
  175.4 0.0 reduce-scatter.4.cloned.1.call-done
  175.4 1.3 copy.22
  176.7 0.0 copy-start.1
  176.7 2.7 %scatter_custom_fusion.1 = bf16[832,640]{0,1:T(8,128)(2,1)} fusion(s32[256]{0:T(256)S(1)} %compare_select_fusion.1, bf16[]{:T(256)} %constant.40.clone.1, bf16[832,256]{0,1:T(8,128)(2,1)S(1)} %copy.22, f32[832]{0:T(1024)S(1)} %convert_element_type.40), kind=kCustom, calls=%fused_computation.16 | custom fusion | flops 638976 | bytes 1527810 | tf_op jit(solution)/shard_map/scatter | solution.py:46
  179.4 3.2 %all-to-all-done = s32[1,16,40]{2,0,1:T(1,128)S(1)} async-done(((s32[1,16,40]{2,0,1:T(1,128)}), s32[1,16,40]{2,0,1:T(1,128)S(1)}, u32[]{:S(2)}, u32[]{:S(2)}) %all-to-all-start) | async-done | bytes 2592 | tf_op jit(solution)/shard_map/all_to_all | solution.py:59
  182.6 3.7 %all-to-all-start.1 = ((bf16[832,16,40]{0,2,1:T(8,128)(2,1)}), bf16[832,16,40]{0,2,1:T(8,128)(2,1)S(1)}, u32[]{:S(2)}, u32[]{:S(2)}) async-start(bf16[832,16,40]{0,2,1:T(8,128)(2,1)} %bitcast.5), calls=%async_computation.1 | async-start | bytes 2293760 | tf_op jit(solution)/shard_map/all_to_all | solution.py:52
  186.3 0.0 copy-done.1
  186.3 0.4 copy.19
  186.7 0.5 broadcast.83
  187.2 0.7 reduce.7
  187.9 0.1 reshape.68
  188.0 24.7 %all-to-all-done.1 = bf16[832,16,40]{0,2,1:T(8,128)(2,1)S(1)} async-done(((bf16[832,16,40]{0,2,1:T(8,128)(2,1)}), bf16[832,16,40]{0,2,1:T(8,128)(2,1)S(1)}, u32[]{:S(2)}, u32[]{:S(2)}) %all-to-all-start.1) | async-done | bytes 1064992 | tf_op jit(solution)/shard_map/all_to_all | solution.py:52
  212.7 6.2 %scatter_fusion = bf16[832,384]{0,1:T(8,128)(2,1)S(1)} fusion(bf16[832,384]{0,1:T(8,128)(2,1)S(1)} %copy.19, s32[640]{0:T(1024)S(1)} %fusion.17, bf16[640,832]{1,0:T(8,128)(2,1)S(1)} %bitcast.36), kind=kCustom, calls=%fused_computation.2 | custom fusion | bytes 3197440 | tf_op jit(solution)/shard_map/scatter | solution.py:63
  219.0 1.1 copy.20
  (9 shorter events, 0.1 us)
Async XLA Ops:
  6.5 6.5 %copy-start = (bf16[832,1024]{1,0:T(8,128)(2,1)S(1)}, bf16[832,1024]{1,0:T(8,128)(2,1)}, u32[]{:S(2)}) copy-start(bf16[832,1024]{1,0:T(8,128)(2,1)} %param.7) | copy-start | bytes 5111812
  6.5 152.2 %all-gather.2.cloned.1.call-start = ((), (), s32[]{:S(2)}) async-start(), calls=%async_computation.3 | async-start | bytes 12673024 | tf_op jit(solution)/shard_map/all_gather | solution.py:28
  7.3 168.2 %reduce-scatter.4.cloned.1.call-start = ((), (), s32[]{:S(2)}) async-start(), calls=%async_computation.4 | async-start | bytes 1277952
  167.2 1.3 copy-start.3
  167.2 8.2 %copy-start.2 = (bf16[832]{0:T(1024)(128)(2,1)S(1)}, bf16[832]{0:T(1024)(128)(2,1)}, u32[]{:S(2)}) copy-start(bf16[832]{0:T(1024)(128)(2,1)} %param.11) | copy-start | bytes 4996
  171.6 11.0 %all-to-all-start = ((s32[1,16,40]{2,0,1:T(1,128)}), s32[1,16,40]{2,0,1:T(1,128)S(1)}, u32[]{:S(2)}, u32[]{:S(2)}) async-start(s32[1,16,40]{2,0,1:T(1,128)} %reshape.67), calls=%async_computation | async-start | bytes 16384 | tf_op jit(solution)/shard_map/all_to_all | solution.py:59
  176.7 9.6 %copy-start.1 = (bf16[832,384]{1,0:T(8,128)(2,1)S(1)}, bf16[832,384]{1,0:T(8,128)(2,1)}, u32[]{:S(2)}) copy-start(bf16[832,384]{1,0:T(8,128)(2,1)} %param.13) | copy-start | bytes 1916932
  182.6 30.1 %all-to-all-start.1 = ((bf16[832,16,40]{0,2,1:T(8,128)(2,1)}), bf16[832,16,40]{0,2,1:T(8,128)(2,1)S(1)}, u32[]{:S(2)}, u32[]{:S(2)}) async-start(bf16[832,16,40]{0,2,1:T(8,128)(2,1)} %bitcast.5), calls=%async_computation.1 | async-start | bytes 2293760 | tf_op jit(solution)/shard_map/all_to_all | solution.py:52
Sparse Core Ops, SparseCore 0:
  10.1 148.5 all-gather.1
  168.6 6.5 reduce-scatter.3
where the time goes:
time: 228 us; the launch traced here: 227 us
  waiting for transfers between devices  167 us (73%)
  local copies, waits for them, and re-layouts  16.4 us (7%)
  between operations  13.6 us (6%)
  matrix products  8.46 us (4%)
  other arithmetic  8.4 us (4%)
  starting transfers between devices  7.56 us (3%)
  blocking collectives  5.06 us (2%)
    all_gather x1, waiting for transfers between devices, shards(): lax.all_gather(merge_weight, 'seq', axis=2, tiled=True)  139 us
    all_to_all x1, waiting for transfers between devices, shards(): lax.all_to_all(send_rows.reshape(feat_width, seq_count, capacity), 'seq',...  24.7 us
    dot_general x1, matrix products, shards(): jnp.einsum('fmk,kfc->cm', grouped, lax.all_gather(merge_weight, 'seq', ax...  8.46 us
    scatter x2, local copies, waits for them, and re-layouts, shards(): text_embed.at[:, got_pos.reshape(-1)]  7.36 us
  transfers between devices with their start and end apart: 4, of which 3 were waited for; matrix products, arithmetic and copies ran while one was open for 7% of the time, Pallas kernels for 0%

commit v1 on v0

v1 whole, which is shorter than its diff:
```python
import jax
import jax.numpy as jnp
from jax import lax
from jax.sharding import PartitionSpec as P

D = 1664
GROUP = 4


def norm_rows(patches, ln_gain, ln_bias):
    values = patches.astype(jnp.float32)
    width = values.shape[0]
    own_mean = jnp.sum(values, axis=0) / width
    own_dev = values - own_mean[None, :]
    own_square = jnp.sum(own_dev * own_dev, axis=0)
    stats = lax.all_gather(jnp.stack([own_mean, own_square]), "tp", axis=0)
    row_mean = jnp.mean(stats[:, 0], axis=0)
    apart = stats[:, 0] - row_mean[None, :]
    row_var = (jnp.sum(stats[:, 1], axis=0) + width * jnp.sum(apart * apart, axis=0)) / D
    scaled = (values - row_mean[None, :]) * lax.rsqrt(row_var + 1e-06)[None, :] * ln_gain.astype(
        jnp.float32
    )[:, None] + ln_bias.astype(jnp.float32)[:, None]
    return scaled.astype(jnp.bfloat16)


def shards(patches, ln_gain, ln_bias, merge_weight, merge_bias, targets, text_embed):
    seq_count = lax.axis_size("seq")
    planes = [[g + j for j in range(GROUP)] for g in range(0, seq_count, GROUP)]
    columns = [list(range(j, seq_count, GROUP)) for j in range(GROUP)]
    feat_width = patches.shape[0]
    merged_rows = patches.shape[1] // GROUP
    prompt_rows = text_embed.shape[1]
    capacity = 5 * merged_rows // (2 * seq_count)

    weight_part = lax.all_to_all(
        merge_weight, "seq", split_axis=0, concat_axis=2, axis_index_groups=planes, tiled=True
    )[0]
    weight = lax.all_gather(weight_part, "seq", axis=1, axis_index_groups=columns, tiled=True)
    all_targets = lax.all_gather(targets, "seq", axis=0)

    normed = norm_rows(patches, ln_gain, ln_bias)
    by_patch = normed.reshape(feat_width, merged_rows, GROUP).transpose(2, 0, 1)
    tokens = lax.all_to_all(
        by_patch, "seq", split_axis=0, concat_axis=0, axis_index_groups=planes, tiled=True
    )
    target_dev = targets // prompt_rows
    earlier = jnp.arange(merged_rows)[:, None] < jnp.arange(merged_rows)[None, :]
    order_in = jnp.sum((earlier & (target_dev[:, None] == target_dev[None, :])).astype(jnp.int32), axis=0)
    slot_index = target_dev * capacity + order_in
    pick = (jnp.arange(seq_count * capacity)[:, None] == slot_index[None, :]).astype(jnp.bfloat16)
    me = lax.axis_index("seq")
    mine = (all_targets // prompt_rows) == me
    rank = jnp.dot(
        mine.astype(jnp.bfloat16), earlier.astype(jnp.bfloat16), preferred_element_type=jnp.float32
    ).astype(jnp.int32)
    in_slot = mine[:, None, :] & (rank[:, None, :] == jnp.arange(capacity)[None, :, None])
    got_pos = jnp.sum(in_slot * (all_targets % prompt_rows + 1)[:, None, :], axis=2).reshape(-1) - 1
    place = got_pos[:, None] == jnp.arange(prompt_rows)[None, :]
    hit = jnp.any(place, axis=0)

    partial_terms = jnp.einsum(
        "sfm,fc->scm", tokens, weight, preferred_element_type=jnp.float32
    ).astype(jnp.bfloat16)
    halves = lax.psum_scatter(partial_terms, "tp", scatter_dimension=1, tiled=True)
    parts = lax.all_to_all(
        halves, "seq", split_axis=0, concat_axis=0, axis_index_groups=planes, tiled=True
    )
    merged = (
        jnp.sum(parts.astype(jnp.float32), axis=0) + merge_bias.astype(jnp.float32)[:, None]
    ).astype(jnp.bfloat16)
    send = jnp.einsum("sm,cm->sc", pick, merged, preferred_element_type=jnp.float32).astype(jnp.bfloat16)
    got = lax.all_to_all(
        send.reshape(seq_count, capacity, feat_width), "seq", split_axis=0, concat_axis=0, tiled=True
    ).reshape(seq_count * capacity, feat_width)
    image = jnp.einsum(
        "sc,sp->cp", got, place.astype(jnp.bfloat16), preferred_element_type=jnp.float32
    ).astype(jnp.bfloat16)
    return jnp.where(hit[None, :], image, text_embed)


def solution(mesh):
    in_specs = (
        P("tp", "seq"),
        P("tp"),
        P("tp"),
        P(None, "tp", "seq"),
        P("tp"),
        P("seq"),
        P("tp", "seq"),
    )
    out_specs = P("tp", "seq")
    return jax.shard_map(shards, mesh=mesh, in_specs=in_specs, out_specs=out_specs, check_vma=False)
```

time: 228 us -> 216 us (0.947)
  waiting for transfers between devices: 167 us -> 67.6 us
  blocking collectives: 5.06 us -> 95.6 us
  other arithmetic: 8.4 us -> 2.57 us
  starting transfers between devices: 7.56 us -> 9.88 us
    all_gather x1, waiting for transfers between devices: 139 us -> 25.9 us  [shards(): lax.all_gather(weight_part, 'seq', axis=1, axis_index_groups=columns, til...]
    all_gather x0 -> x2, blocking collectives: none -> 53.7 us  [the longest x1 51.9 us: shards(): all_targets = lax.all_gather(targets, 'seq', axis=0)]
    all_to_all x0 -> x2, blocking collectives: none -> 41.9 us  [the longest x1 25 us: shards(): lax.all_to_all(by_patch, 'seq', split_axis=0, concat_axis=0, axis_index_g...]
    unnamed x3, waiting for transfers between devices: 0.75 us -> 20.7 us
    scatter x3 -> x0, local copies, waits for them, and re-layouts: 8.77 us -> none  [the longest x2 7.36 us: shards(): text_embed.at[:, got_pos.reshape(-1)]]
    all_to_all x2, waiting for transfers between devices: 27.9 us -> 21 us  [the longest x1 21 us: shards(): lax.all_to_all(halves, 'seq', split_axis=0, concat_axis=0, axis_index_gro...]
    convert_element_type x1 -> x3, local copies, waits for them, and re-layouts: 1.69 us -> 7.83 us  [the longest x1 4.39 us: shards(): partial_terms = jnp.einsum('sfm,fc->scm', tokens, weight, preferred_eleme...]
    psum x2 -> x0, blocking collectives: 5.06 us -> none  [the longest x1 2.59 us: shards(): feature_total = lax.psum(jnp.sum(values, axis=0), 'tp')]
  transfers between devices with their start and end apart: 4 -> 4, of which waited for: 3 -> 3; matrix products, arithmetic and copies ran while one was open for 7% -> 4% of each run, Pallas kernels for 0% -> 0%
where the time goes in v1:
time: 216 us
  blocking collectives  95.6 us (44%)
  waiting for transfers between devices  67.6 us (31%)
  local copies, waits for them, and re-layouts  17.3 us (8%)
  between operations  14.3 us (7%)
  starting transfers between devices  9.88 us (5%)
  matrix products  8.76 us (4%)
  other arithmetic  2.57 us (1%)
    all_gather x1, blocking collectives, shards(): all_targets = lax.all_gather(targets, 'seq', axis=0)  51.9 us
    all_gather x1, waiting for transfers between devices, shards(): lax.all_gather(weight_part, 'seq', axis=1, axis_index_groups=columns, til...  25.9 us
    all_to_all x1, blocking collectives, shards(): lax.all_to_all(by_patch, 'seq', split_axis=0, concat_axis=0, axis_index_g...  25 us
    all_to_all x1, waiting for transfers between devices, shards(): lax.all_to_all(halves, 'seq', split_axis=0, concat_axis=0, axis_index_gro...  21 us
    unnamed x3, waiting for transfers between devices  20.7 us
    all_to_all x1, blocking collectives, shards(): lax.all_to_all(merge_weight, 'seq', split_axis=0, concat_axis=2, axis_ind...  16.9 us
    dot_general x1, matrix products, shards(): jnp.einsum('sfm,fc->scm', tokens, weight, preferred_element_type=jnp.floa...  6.34 us
    all_to_all x1, starting transfers between devices, shards(): lax.all_to_all(send.reshape(seq_count, capacity, feat_width), 'seq', spli...  5.79 us
  transfers between devices with their start and end apart: 4, of which 3 were waited for; matrix products, arithmetic and copies ran while one was open for 4% of the time, Pallas kernels for 0%

profile of v1, /device:TPU:0, one launch (start us, length us, event | category | flops | bytes accessed | tf_op | source)
XLA Modules:
  0.0 216.0 jit_solution(2334883575974829876)
XLA Ops:
  6.5 0.0 copy-start.2
  6.5 0.0 copy-start.3
  6.5 0.0 copy-start
  6.5 0.0 all-gather.6.cloned.1.call-start
  6.5 16.9 %all_to_all.30 = bf16[4,832,104]{1,2,0:T(8,128)(2,1)} all-to-all(bf16[4,832,104]{1,2,0:T(8,128)(2,1)} %param.10), channel_id=1, replica_groups={{0,2,4,6},{8,10,12,14},{16,18,20,22},{24,26,28,30},{1,3,5,7},{9,11,13,1..., dimensions={0} | all-to-all | bytes 1384448 | tf_op jit(solution)/shard_map/all_to_all | solution.py:35
  23.5 0.0 all-gather.6.cloned.1.call-update
  23.5 0.0 all-reduce.3.cloned.1.call-start
  23.5 0.0 copy-done.2
  23.6 0.0 copy-done.3
  23.6 0.0 copy-done
  23.6 0.3 convert_reduce_fusion
  23.9 0.5 fusion.1
  24.4 1.8 all-gather.3
  26.3 0.7 fusion.5
  27.0 1.7 copy.27
  28.7 1.5 reshape.49
  30.2 3.2 %copy.28 = bf16[4,832,256]{2,1,0:T(8,128)(2,1)S(1)} copy(bf16[4,832,256]{1,0,2:T(4,128)(2,1)} %bitcast.50) | data formatting | bytes 3407872 | tf_op jit(solution)/shard_map/transpose | solution.py:42
  33.3 25.0 %all_to_all.31 = bf16[4,832,256]{2,1,0:T(8,128)(2,1)} all-to-all(bf16[4,832,256]{2,1,0:T(8,128)(2,1)S(1)} %copy.28), channel_id=1, replica_groups={{0,2,4,6},{8,10,12,14},{16,18,20,22},{24,26,28,30},{1,3,5,7},{9,11,13,1..., dimensions={0} | all-to-all | bytes 3407872 | tf_op jit(solution)/shard_map/all_to_all | solution.py:43
  58.3 25.9 %all-gather.6.cloned.1.call-done = bf16[832,1664]{0,1:T(8,128)(2,1)} async-done(((bf16[832,416]{0,1:T(8,128)(2,1)}), bf16[832,1664]{0,1:T(8,128)(2,1)}) %all-gather.6.cloned.1.call-update) | async-done | bytes 2768912 | tf_op jit(solution)/shard_map/all_gather | solution.py:38
  84.3 6.3 %fusion.6 = bf16[4,1664,256]{1,2,0:T(8,128)(2,1)S(1)} fusion(bf16[4,832,256]{2,1,0:T(8,128)(2,1)} %all_to_all.31, bf16[832,1664]{0,1:T(8,128)(2,1)} %all-gather.6.cloned.1.call-done), kind=kOutput, calls=%fused_computation.11 | convolution fusion | flops 2837053440 | bytes 7880704 | tf_op jit(solution)/shard_map/sfm,fc->scm/dot_general | solution.py:61
  90.6 4.4 %copy.29 = bf16[4,1664,256]{2,0,1:T(4,128)(2,1)} copy(bf16[4,1664,256]{1,2,0:T(8,128)(2,1)S(1)} %fusion.6) | data formatting | bytes 6815744 | tf_op jit(solution)/shard_map/convert_element_type | solution.py:63
  95.0 0.0 copy-start.6
  95.0 0.0 all-reduce.3.cloned.1.call-update
  95.0 0.6 copy-done.6
  95.6 0.6 dynamic-slice
  96.9 20.7 %all-reduce.3.cloned.1.call-done = bf16[4,1664,256]{2,0,1:T(4,128)(2,1)} async-done(((bf16[4,1664,256]{2,0,1:T(4,128)(2,1)}), bf16[4,1664,256]{2,0,1:T(4,128)(2,1)}) %all-reduce.3.cloned.1.call-update) | async-done | bytes 3407888
  117.6 2.0 constant_dynamic-slice_fusion
  119.6 1.4 copy.30
  121.0 0.0 copy-start.4
  121.0 0.0 copy-start.1
  121.0 4.0 %all-to-all-start.2 = ((bf16[4,832,256]{2,1,0:T(8,128)(2,1)}), bf16[4,832,256]{2,1,0:T(8,128)(2,1)S(1)}, u32[]{:S(2)}, u32[]{:S(2)}) async-start(bf16[4,832,256]{2,1,0:T(8,128)(2,1)} %copy.30), calls=%async_computation.2 | async-start | bytes 3407872 | tf_op jit(solution)/shard_map/all_to_all | solution.py:65
  125.1 0.0 copy-done.4
  125.1 0.0 copy-done.1
  125.1 0.1 convert_reduce_fusion.2
  125.2 21.0 %all-to-all-done.2 = bf16[4,832,256]{2,1,0:T(8,128)(2,1)S(1)} async-done(((bf16[4,832,256]{2,1,0:T(8,128)(2,1)}), bf16[4,832,256]{2,1,0:T(8,128)(2,1)S(1)}, u32[]{:S(2)}, u32[]{:S(2)}) %all-to-all-start.2) | async-done | bytes 1703968 | tf_op jit(solution)/shard_map/all_to_all | solution.py:65
  146.2 0.2 convert_reduce_fusion.1
  146.4 0.5 convolution_convert_fusion.1
  147.0 0.0 copy-start.5
  147.0 1.8 copy.31
  148.7 5.8 %all-to-all-start.3 = ((bf16[16,40,832]{2,1,0:T(8,128)(2,1)}), bf16[16,40,832]{2,1,0:T(8,128)(2,1)S(1)}, u32[]{:S(2)}, u32[]{:S(2)}) async-start(bf16[16,40,832]{2,1,0:T(8,128)(2,1)} %bitcast.12), calls=%async_computation.3 | async-start | bytes 2293760 | tf_op jit(solution)/shard_map/all_to_all | solution.py:72
  154.6 51.9 %all-gather.2 = s32[16,1,256]{2,1,0:T(1,128)S(1)} all-gather(s32[1,1,256]{2,1,0:T(1,128)S(1)} %bitcast.55), channel_id=2, replica_groups=mesh['seq'=16,'tp'=2] {'seq'}, dimensions={0}, use_global_device_ids=true | all-gather | bytes 17408 | tf_op jit(solution)/shard_map/all_gather | solution.py:39
  206.5 0.2 convolution_convert_fusion.3
  206.7 0.4 select_reduce_fusion
  207.1 0.1 sub.44
  207.2 0.2 fusion.9
  207.4 0.0 all-to-all-done.3
  207.4 0.0 copy-done.5
  207.4 1.7 fusion.8
  (15 shorter events, 0.2 us)
Async XLA Ops:
  6.5 17.0 %copy-start.2 = (bf16[832]{0:T(1024)(128)(2,1)S(1)}, bf16[832]{0:T(1024)(128)(2,1)}, u32[]{:S(2)}) copy-start(bf16[832]{0:T(1024)(128)(2,1)} %param.8) | copy-start | bytes 4996
  6.5 17.0 %copy-start.3 = (bf16[832]{0:T(1024)(128)(2,1)S(1)}, bf16[832]{0:T(1024)(128)(2,1)}, u32[]{:S(2)}) copy-start(bf16[832]{0:T(1024)(128)(2,1)} %param.9) | copy-start | bytes 4996
  6.5 17.0 %copy-start = (bf16[832,1024]{1,0:T(8,128)(2,1)S(1)}, bf16[832,1024]{1,0:T(8,128)(2,1)}, u32[]{:S(2)}) copy-start(bf16[832,1024]{1,0:T(8,128)(2,1)} %param.7) | copy-start | bytes 5111812
  6.5 77.7 %all-gather.6.cloned.1.call-start = ((), (), s32[]{:S(2)}) async-start(), calls=%async_computation.4 | async-start | bytes 3727360 | tf_op jit(solution)/shard_map/all_gather | solution.py:38
  23.5 94.1 %all-reduce.3.cloned.1.call-start = ((), (), s32[]{:S(2)}) async-start(), calls=%async_computation.5 | async-start | bytes 6815744
  95.0 0.7 copy-start.6
  121.0 4.1 %copy-start.4 = (bf16[832]{0:T(1024)(128)(2,1)S(1)}, bf16[832]{0:T(1024)(128)(2,1)}, u32[]{:S(2)}) copy-start(bf16[832]{0:T(1024)(128)(2,1)} %param.11) | copy-start | bytes 4996
  121.0 4.1 %copy-start.1 = (s32[256]{0:T(256)S(1)}, s32[256]{0:T(256)}, u32[]{:S(2)}) copy-start(s32[256]{0:T(256)} %param.12) | copy-start | bytes 3076
  121.0 25.2 %all-to-all-start.2 = ((bf16[4,832,256]{2,1,0:T(8,128)(2,1)}), bf16[4,832,256]{2,1,0:T(8,128)(2,1)S(1)}, u32[]{:S(2)}, u32[]{:S(2)}) async-start(bf16[4,832,256]{2,1,0:T(8,128)(2,1)} %copy.30), calls=%async_computation.2 | async-start | bytes 3407872 | tf_op jit(solution)/shard_map/all_to_all | solution.py:65
  147.0 60.4 %copy-start.5 = (bf16[832,384]{1,0:T(8,128)(2,1)S(1)}, bf16[832,384]{1,0:T(8,128)(2,1)}, u32[]{:S(2)}) copy-start(bf16[832,384]{1,0:T(8,128)(2,1)} %param.13) | copy-start | bytes 1916932
  148.7 58.6 %all-to-all-start.3 = ((bf16[16,40,832]{2,1,0:T(8,128)(2,1)}), bf16[16,40,832]{2,1,0:T(8,128)(2,1)S(1)}, u32[]{:S(2)}, u32[]{:S(2)}) async-start(bf16[16,40,832]{2,1,0:T(8,128)(2,1)} %bitcast.12), calls=%async_computation.3 | async-start | bytes 2293760 | tf_op jit(solution)/shard_map/all_to_all | solution.py:72
Sparse Core Ops, SparseCore 0:
  23.6 60.6 all-gather.5
  95.1 22.3 all-reduce.2

commit v2 on v0

v2 whole, which is shorter than its diff:
```python
import functools

import jax
import jax.numpy as jnp
from jax import lax
from jax.experimental import pallas as pl
from jax.experimental.pallas import tpu as pltpu
from jax.sharding import PartitionSpec as P

D = 1664
GROUP = 4
LANES = 128
MESH = pl.DeviceIdType.MESH
F32 = jnp.float32
BF16 = jnp.bfloat16


def contract(lhs, rhs, lhs_dim, rhs_dim):
    return lax.dot_general(
        lhs, rhs, (((lhs_dim,), (rhs_dim,)), ((), ())), preferred_element_type=F32
    )


def packing(columns, feats):
    main = columns // LANES * LANES
    rest = columns - main
    if main and rest and LANES % rest == 0 and feats % (16 * (LANES // rest)) == 0:
        return main, LANES // rest
    return columns, 0


def merge_kernel(
    nseq, ntp, capacity, slots,
    x_ref, gain_ref, bias_ref, w_ref, mbias_ref, trow_ref, tcol_ref, text_ref,
    out_ref,
    stats, xs, tok, wpl, wmain, wrem, psend, parts, merged, pick, posend, posbuf, send, got, place,
    s_w, r_w, s_z, r_z, s_t, r_t, s_st, r_st, s_p, r_p, s_d, r_d, s_pos, r_pos,
):
    me, tp = lax.axis_index("seq"), lax.axis_index("tp")
    plane, member = me // GROUP, lax.rem(me, GROUP)
    planes = nseq // GROUP
    owned = planes // ntp
    feats, tokens = x_ref.shape
    rows = tokens // GROUP
    prompt_rows = text_ref.shape[1]
    block_cols = wpl.shape[2] * GROUP
    main, fold = packing(block_cols, feats)

    def remote(src, dst, send_sem, recv_sem, seq_id, tp_id):
        return pltpu.make_async_remote_copy(
            src_ref=src, dst_ref=dst, send_sem=send_sem, recv_sem=recv_sem,
            device_id=(seq_id, tp_id), device_id_type=MESH,
        )

    barrier = pltpu.get_barrier_semaphore()

    @pl.loop(0, nseq)
    def _(other):
        @pl.when(other != me)
        def _():
            pl.semaphore_signal(barrier, inc=1, device_id=(other, tp), device_id_type=MESH)

    for other_tp in range(ntp):
        @pl.when(other_tp != tp)
        def _():
            for i in range(GROUP):
                pl.semaphore_signal(
                    barrier, inc=1, device_id=(plane * GROUP + i, other_tp), device_id_type=MESH
                )
    pl.semaphore_wait(barrier, nseq - 1 + GROUP * (ntp - 1))

    def weight_copy(i):
        return remote(
            w_ref.at[i], wpl.at[member], s_w.at[i], r_w.at[member], plane * GROUP + i, tp
        )

    def weight_arrival(i):
        return remote(w_ref.at[i], wpl.at[i], s_w.at[i], r_w.at[i], plane * GROUP + i, tp)

    for i in range(GROUP):
        @pl.when(i != member)
        def _():
            weight_copy(i).start()
    wpl[member] = w_ref[member]

    chunk = 256

    @pl.loop(0, tokens // chunk)
    def _(c):
        at = pl.ds(pl.multiple_of(c * chunk, chunk), chunk)
        values = x_ref[:, at].astype(F32)
        mean = jnp.sum(values, axis=0, keepdims=True) / feats
        apart = values - mean
        stats[tp, 0:1, at] = mean
        stats[tp, 1:2, at] = jnp.sum(apart * apart, axis=0, keepdims=True)

    def stats_copy(other_tp, slot):
        return remote(
            stats.at[slot], stats.at[slot], s_st.at[other_tp], r_st.at[slot], me, other_tp
        )

    for other_tp in range(ntp):
        @pl.when(other_tp != tp)
        def _():
            stats_copy(other_tp, tp).start()

    for i in range(GROUP):
        @pl.when(i != member)
        def _():
            weight_arrival(i).wait_recv()
    block = jnp.concatenate([wpl[i] for i in range(GROUP)], axis=1)
    if fold:
        wmain[plane] = block[:, :main]
        part = feats // fold
        wrem[plane] = jnp.concatenate(
            [block[q * part : (q + 1) * part, main:] for q in range(fold)], axis=1
        )
    else:
        wmain[plane] = block

    def relay(zz, up):
        target = (plane + 1 if up else plane - 1) * GROUP + member
        way = 1 if up else 0
        copies = [remote(wmain.at[zz], wmain.at[zz], s_z.at[way, zz, 0], r_z.at[zz, 0], target, tp)]
        if fold:
            copies.append(
                remote(wrem.at[zz], wrem.at[zz], s_z.at[way, zz, 1], r_z.at[zz, 1], target, tp)
            )
        return copies

    def pass_on(zz, act):
        @pl.when((zz <= plane) & (plane + 1 < planes))
        def _():
            for copy in relay(zz, True):
                act(copy)

        @pl.when((zz >= plane) & (plane > 0))
        def _():
            for copy in relay(zz, False):
                act(copy)

    pass_on(plane, lambda copy: copy.start())

    for other_tp in range(ntp):
        @pl.when(other_tp != tp)
        def _():
            stats_copy(other_tp, other_tp).wait_recv()
    wide = GROUP * LANES
    from_tok = lax.broadcasted_iota(jnp.int32, (wide, wide), 0)
    to_tok = lax.broadcasted_iota(jnp.int32, (wide, wide), 1)
    sorter = (from_tok == GROUP * (to_tok % LANES) + to_tok // LANES).astype(F32).astype(BF16)
    for c in range(tokens // wide):
        at = slice(c * wide, (c + 1) * wide)
        mean = sum(stats[q, 0:1, at] for q in range(ntp)) / ntp
        square = sum(
            stats[q, 1:2, at] + feats * (stats[q, 0:1, at] - mean) ** 2 for q in range(ntp)
        )
        scale = lax.rsqrt(square / (feats * ntp) + 1e-06)
        normed = (
            (x_ref[:, at].astype(F32) - mean) * scale * gain_ref[...] + bias_ref[...]
        ).astype(BF16)
        by_patch = jnp.dot(normed, sorter, preferred_element_type=F32).astype(BF16)
        for i in range(GROUP):
            xs[i, :, c * LANES : (c + 1) * LANES] = by_patch[:, i * LANES : (i + 1) * LANES]

    def token_copy(i, slot, sem):
        return remote(xs.at[i], tok.at[slot], s_t.at[i], r_t.at[sem], plane * GROUP + i, tp)

    for i in range(GROUP):
        @pl.when(i != member)
        def _():
            token_copy(i, member, member).start()
    tok[member] = xs[member]

    dest_row = trow_ref[...] // prompt_rows
    dest_col = tcol_ref[...] // prompt_rows
    first = lax.broadcasted_iota(jnp.int32, (rows, rows), 0)
    second = lax.broadcasted_iota(jnp.int32, (rows, rows), 1)
    same = dest_col == dest_row
    order_row = jnp.sum((same & (first < second)).astype(F32), axis=0, keepdims=True)
    order_col = jnp.sum((same & (second < first)).astype(F32), axis=1, keepdims=True)
    slot_row = dest_row * slots + order_row.astype(jnp.int32)
    slot_col = dest_col * slots + order_col.astype(jnp.int32)
    local_col = (tcol_ref[...] - dest_col * prompt_rows + 1).astype(F32)

    def pos_copy(other, slot):
        return remote(
            posend.at[other], posbuf.at[slot], s_pos.at[other], r_pos.at[slot], other, tp
        )

    @pl.loop(0, nseq)
    def _(other):
        base = other * slots
        slot_at = base + lax.broadcasted_iota(jnp.int32, (slots, rows), 0)
        pick[pl.ds(pl.multiple_of(base, 16), slots), :] = (
            (slot_at == slot_row).astype(F32).astype(BF16)
        )
        lane = lax.broadcasted_iota(jnp.int32, (rows, LANES), 1)
        held = jnp.where((slot_col == base + lane) & (lane < slots), local_col, 0.0)
        posend[other] = jnp.broadcast_to(jnp.sum(held, axis=0, keepdims=True), (8, LANES))

        @pl.when(other != me)
        def _():
            pos_copy(other, me).start()

        @pl.when(other == me)
        def _():
            posbuf[me] = posend[me]

    for i in range(GROUP):
        @pl.when(i != member)
        def _():
            token_copy(i, i, i).wait_recv()

    def part_copy(zz, i):
        home = zz // owned
        return remote(
            psend.at[zz, i],
            parts.at[zz - home * owned, member * ntp + tp],
            s_p.at[zz, i],
            r_p.at[zz - home * owned, member * ntp + tp],
            plane * GROUP + i,
            home,
        )

    def here(zz, i):
        return (zz // owned == tp) & (i == member)

    def use_block(zz):
        if fold:
            lanes = LANES // fold
            rest = jnp.concatenate(
                [wrem[zz][:, q * lanes : (q + 1) * lanes] for q in range(fold)], axis=0
            )
            weight = jnp.concatenate([wmain[zz], rest], axis=1)
        else:
            weight = wmain[zz]
        for i in range(GROUP):
            psend[zz, i] = contract(weight, tok[i], 0, 0).astype(BF16)

            @pl.when(jnp.logical_not(here(zz, i)))
            def _():
                part_copy(zz, i).start()

            @pl.when(here(zz, i))
            def _():
                parts[zz - tp * owned, member * ntp + tp] = psend[zz, i]

    def row_copy(other, slot):
        return remote(
            send.at[other], got.at[slot], s_d.at[other], r_d.at[slot], other, tp
        )

    def part_arrival(b, i, q):
        return remote(
            psend.at[0, 0], parts.at[b, i * ntp + q], s_p.at[0, 0], r_p.at[b, i * ntp + q], me, q
        )

    def place_rows():
        for b in range(owned):
            total = jnp.zeros((block_cols, rows), F32)
            for i in range(GROUP):
                for q in range(ntp):
                    @pl.when((i != member) | (q != tp))
                    def _():
                        part_arrival(b, i, q).wait_recv()
                    total = total + parts[b, i * ntp + q].astype(F32)
            at = slice(b * block_cols, (b + 1) * block_cols)
            merged[at, :] = (total + mbias_ref[at, :]).astype(BF16)

        @pl.loop(0, planes)
        def _(step):
            to = lax.rem(plane + planes // 2 + step, planes)
            size = GROUP * slots
            picked = contract(
                pick[pl.ds(pl.multiple_of(to * size, 16), size), :], merged[...], 1, 1
            ).astype(BF16)
            for i in range(GROUP):
                other = to * GROUP + i
                send[other] = picked[i * slots : (i + 1) * slots]

                @pl.when(other != me)
                def _():
                    row_copy(other, me).start()

                @pl.when(other == me)
                def _():
                    got[me] = send[me]

    def step_of(zz):
        return jnp.where(zz < plane, 2 * (plane - zz) - 1, 2 * (zz - plane))

    last = jnp.maximum(step_of(tp * owned), step_of(tp * owned + owned - 1))
    ready = jnp.minimum(last + 2, 2 * planes - 2)

    @pl.loop(0, 2 * planes - 1)
    def _(step):
        far = (step + 1) // 2
        zz = jnp.where(lax.rem(step, 2) == 1, plane - far, plane + far)

        @pl.when((zz >= 0) & (zz < planes))
        def _():
            @pl.when(zz != plane)
            def _():
                for copy in relay(zz, True):
                    copy.wait_recv()
                pass_on(zz, lambda copy: copy.start())
            use_block(zz)

        @pl.when(step == ready)
        def _():
            place_rows()

    diagonal = lax.broadcasted_iota(jnp.int32, (slots, LANES), 0) == lax.broadcasted_iota(
        jnp.int32, (slots, LANES), 1
    )
    position = lax.broadcasted_iota(jnp.int32, (slots, prompt_rows), 1).astype(F32) + 1.0

    def spots(other, hits):
        @pl.when(other != me)
        def _():
            pos_copy(other, other).wait_recv()
        line = posbuf[other][0:1]
        column = jnp.sum(jnp.where(diagonal, line, 0.0), axis=1, keepdims=True)
        spot = (column == position).astype(F32)
        place[pl.ds(pl.multiple_of(other * slots, 16), slots), :] = spot.astype(BF16)
        return hits + jnp.sum(spot, axis=0, keepdims=True)

    hits = lax.fori_loop(0, nseq, spots, jnp.zeros((1, prompt_rows), F32))

    @pl.loop(0, nseq)
    def _(other):
        @pl.when(other != me)
        def _():
            row_copy(other, other).wait_recv()

    image = contract(got[...].reshape(nseq * slots, feats), place[...], 0, 0)
    out_ref[...] = jnp.where(hits > 0.5, image.astype(BF16), text_ref[...])

    for i in range(GROUP):
        @pl.when(i != member)
        def _():
            weight_copy(i).wait_send()
            token_copy(i, member, member).wait_send()
    for other_tp in range(ntp):
        @pl.when(other_tp != tp)
        def _():
            stats_copy(other_tp, tp).wait_send()

    @pl.loop(0, planes)
    def _(zz):
        pass_on(zz, lambda copy: copy.wait_send())
        for i in range(GROUP):
            @pl.when(jnp.logical_not(here(zz, i)))
            def _():
                part_copy(zz, i).wait_send()

    @pl.loop(0, nseq)
    def _(other):
        @pl.when(other != me)
        def _():
            pos_copy(other, me).wait_send()
            row_copy(other, me).wait_send()


def shards(patches, ln_gain, ln_bias, merge_weight, merge_bias, targets, text_embed):
    nseq, ntp = lax.axis_size("seq"), lax.axis_size("tp")
    feats, tokens = patches.shape
    rows = tokens // GROUP
    shard_cols = merge_weight.shape[2]
    planes = nseq // GROUP
    owned = planes // ntp
    block_cols = GROUP * shard_cols
    prompt_rows = text_embed.shape[1]
    capacity = 5 * rows // (2 * nseq)
    slots = -(-capacity // 16) * 16
    main, fold = packing(block_cols, feats)
    rem_shape = (planes, feats // fold, LANES) if fold else (1, 16, LANES)
    dma = pltpu.SemaphoreType.DMA
    return pl.pallas_call(
        functools.partial(merge_kernel, nseq, ntp, capacity, slots),
        out_shape=jax.ShapeDtypeStruct(text_embed.shape, text_embed.dtype),
        in_specs=[pl.BlockSpec(memory_space=pltpu.VMEM)] * 8,
        out_specs=pl.BlockSpec(memory_space=pltpu.VMEM),
        scratch_shapes=[
            pltpu.VMEM((ntp, 2, tokens), F32),
            pltpu.VMEM((GROUP, feats, rows), BF16),
            pltpu.VMEM((GROUP, feats, rows), BF16),
            pltpu.VMEM((GROUP, feats, shard_cols), BF16),
            pltpu.VMEM((planes, feats, main), BF16),
            pltpu.VMEM(rem_shape, BF16),
            pltpu.VMEM((planes, GROUP, block_cols, rows), BF16),
            pltpu.VMEM((owned, GROUP * ntp, block_cols, rows), BF16),
            pltpu.VMEM((feats, rows), BF16),
            pltpu.VMEM((nseq * slots, rows), BF16),
            pltpu.VMEM((nseq, 8, LANES), F32),
            pltpu.VMEM((nseq, 8, LANES), F32),
            pltpu.VMEM((nseq, slots, feats), BF16),
            pltpu.VMEM((nseq, slots, feats), BF16),
            pltpu.VMEM((nseq * slots, prompt_rows), BF16),
            dma((GROUP,)), dma((GROUP,)),
            dma((2, planes, 2)), dma((planes, 2)),
            dma((GROUP,)), dma((GROUP,)),
            dma((ntp,)), dma((ntp,)),
            dma((planes, GROUP)), dma((owned, GROUP * ntp)),
            dma((nseq,)), dma((nseq,)),
            dma((nseq,)), dma((nseq,)),
        ],
        compiler_params=pltpu.CompilerParams(
            collective_id=0, has_side_effects=True, vmem_limit_bytes=56 * 2**20
        ),
    )(
        patches,
        ln_gain.astype(F32)[:, None],
        ln_bias.astype(F32)[:, None],
        merge_weight,
        merge_bias.astype(F32)[:, None],
        targets[None, :],
        targets[:, None],
        text_embed,
    )


def solution(mesh):
    in_specs = (
        P("tp", "seq"),
        P("tp"),
        P("tp"),
        P(None, "tp", "seq"),
        P("tp"),
        P("seq"),
        P("tp", "seq"),
    )
    out_specs = P("tp", "seq")
    return jax.shard_map(shards, mesh=mesh, in_specs=in_specs, out_specs=out_specs, check_vma=False)
```

time: 228 us -> 126 us (0.55)
  waiting for transfers between devices: 167 us -> 0 us
  Pallas kernels: 0 us -> 116 us
  between operations: 13.6 us -> 0.01 us
  matrix products: 8.46 us -> 0 us
  other arithmetic: 8.4 us -> 0 us
  starting transfers between devices: 7.56 us -> 0 us
  local copies, waits for them, and re-layouts: 16.4 us -> 9.62 us
  blocking collectives: 5.06 us -> 0 us
    all_gather x1 -> x0, waiting for transfers between devices: 139 us -> none  [shards(): lax.all_gather(merge_weight, 'seq', axis=2, tiled=True)]
    pallas_call x0 -> x1, Pallas kernels: none -> 116 us  [shards(): pl.pallas_call(functools.partial(merge_kernel, nseq, ntp, capacity, slots...]
    all_to_all x2 -> x0, waiting for transfers between devices: 27.9 us -> none  [the longest x1 24.7 us: shards(): lax.all_to_all(send_rows.reshape(feat_width, seq_count, capacity), 'seq',...]
    scatter x3 -> x0, local copies, waits for them, and re-layouts: 8.77 us -> none  [the longest x2 7.36 us: shards(): text_embed.at[:, got_pos.reshape(-1)]]
    dot_general x1 -> x0, matrix products: 8.46 us -> none  [shards(): jnp.einsum('fmk,kfc->cm', grouped, lax.all_gather(merge_weight, 'seq', ax...]
    all_to_all x2 -> x0, starting transfers between devices: 7.52 us -> none  [the longest x1 3.8 us: shards(): lax.all_to_all(send_pos.reshape(1, seq_count, capacity), 'seq', split_axi...]
    broadcast_in_dim x0 -> x4, local copies, waits for them, and re-layouts: none -> 6.39 us  [the longest x1 1.64 us: shards(): merge_bias.astype(F32)[:, None]]
    psum x2 -> x0, blocking collectives: 5.06 us -> none  [the longest x1 2.59 us: shards(): feature_total = lax.psum(jnp.sum(values, axis=0), 'tp')]
  transfers between devices with their start and end apart: 4 -> 0, of which waited for: 3 -> 0; matrix products, arithmetic and copies ran while one was open for 7% -> 0% of each run, Pallas kernels for 0% -> 0%
where the time goes in v2:
time: 126 us
  Pallas kernels  116 us (92%)
  local copies, waits for them, and re-layouts  9.62 us (8%)
    pallas_call x1, Pallas kernels, shards(): pl.pallas_call(functools.partial(merge_kernel, nseq, ntp, capacity, slots...  116 us
    unnamed x4, local copies, waits for them, and re-layouts  3.23 us

profile of v2, /device:TPU:0, one launch (start us, length us, event | category | flops | bytes accessed | tf_op | source)
XLA Modules:
  0.0 125.9 jit_solution(14277488151252298277)
XLA Ops:
  0.0 0.0 copy-start
  0.0 1.5 %copy.13.tcol_ref = s32[256,1]{1,0:T(8,128)} copy(s32[256,1]{0,1:T(1,128)} %bitcast.2) | data formatting | bytes 2048 | tf_op jit(solution)/shard_map/broadcast_in_dim | solution.py:419
  1.5 1.6 %reshape.3.gain_ref = f32[832,1]{1,0:T(8,128)} reshape(bf16[832]{0:T(1024)(128)(2,1)} %param.8) | data formatting | bytes 4992 | tf_op jit(solution)/shard_map/broadcast_in_dim | solution.py:414
  3.1 1.6 %reshape.4.bias_ref = f32[832,1]{1,0:T(8,128)} reshape(bf16[832]{0:T(1024)(128)(2,1)} %param.9) | data formatting | bytes 4992 | tf_op jit(solution)/shard_map/broadcast_in_dim | solution.py:415
  4.8 1.6 %reshape.5.mbias_ref = f32[832,1]{1,0:T(8,128)} reshape(bf16[832]{0:T(1024)(128)(2,1)} %param.11) | data formatting | bytes 4992 | tf_op jit(solution)/shard_map/broadcast_in_dim | solution.py:417
  6.4 0.0 copy-done
  6.4 1.3 copy.11.w_ref
  7.6 116.2 %shard_map.73 = bf16[832,384]{1,0:T(8,128)(2,1)} custom-call(bf16[832,1024]{1,0:T(8,128)(2,1)} %x_ref.1, f32[832,1]{1,0:T(8,128)} %reshape.3.gain_ref, f32[832,1]{1,0:T(8,128)} %reshape.4.bias_ref, bf16[4,832,104]{2,1,0:T(8,128)(2,1)} %copy.11.w_ref, f32[832,1]{1,0:T(8,128)} %reshape.5.mbias_ref, s32[1,256]{1,0:T(1,128)} %bitcast.3, ...), custom_call_target="tpu_custom_call" | custom-call | tf_op jit(solution)/shard_map/pallas_call | solution.py:380
  123.9 2.0 %copy.15 = bf16[832,384]{1,0:T(8,128)(2,1)} copy(bf16[832,384]{1,0:T(8,128)(2,1)} %shard_map.73) | data formatting | bytes 1277952
Async XLA Ops:
  0.0 6.4 %copy-start = (bf16[4,832,104]{1,2,0:T(8,128)(2,1)S(1)}, bf16[4,832,104]{1,2,0:T(8,128)(2,1)}, u32[]{:S(2)}) copy-start(bf16[4,832,104]{1,2,0:T(8,128)(2,1)} %param.10) | copy-start | bytes 2076676

commit v3 on v2

v3 whole, which is shorter than its diff:
```python
import functools

import jax
import jax.numpy as jnp
from jax import lax
from jax.experimental import pallas as pl
from jax.experimental.pallas import tpu as pltpu
from jax.sharding import PartitionSpec as P

D = 1664
GROUP = 4
LANES = 128
MESH = pl.DeviceIdType.MESH
F32 = jnp.float32
BF16 = jnp.bfloat16


def contract(lhs, rhs, lhs_dim, rhs_dim):
    return lax.dot_general(
        lhs, rhs, (((lhs_dim,), (rhs_dim,)), ((), ())), preferred_element_type=F32
    )


def round_up(value, unit):
    return -(-value // unit) * unit


def chunks_of(block_cols):
    first = (block_cols // LANES + 1) // 2 * LANES
    if first and first < block_cols and first % 32 == 0 and block_cols % 32 == 0:
        return [(0, first), (first, block_cols - first)]
    return [(0, block_cols)]


def folding(feats, block_cols):
    main = feats // LANES * LANES
    rest = feats - main
    if main and rest and LANES % rest == 0:
        fold = LANES // rest
        if all(size % (16 * fold) == 0 for _, size in chunks_of(block_cols)):
            return main, fold
    return feats, 0


def payload_rows(slots, size):
    full, rest = divmod(size, LANES)
    total = full * slots
    if rest:
        fold = LANES // rest if LANES % rest == 0 else 1
        total += 8 * (-(-(slots // 8) // fold))
    return round_up(total, 16)


def pack_rows(rows, slots, size):
    full, rest = divmod(size, LANES)
    parts = [rows[:, q * LANES : (q + 1) * LANES] for q in range(full)]
    if rest:
        fold = LANES // rest if LANES % rest == 0 else 1
        groups = [rows[8 * g : 8 * g + 8, full * LANES :] for g in range(slots // 8)]
        for g in range(0, len(groups), fold):
            line = groups[g : g + fold]
            short = LANES - rest * len(line)
            if short:
                line = line + [jnp.zeros((8, short), F32)]
            parts.append(jnp.concatenate(line, axis=1))
    have = sum(part.shape[0] for part in parts)
    if have < payload_rows(slots, size):
        parts.append(jnp.zeros((payload_rows(slots, size) - have, LANES), F32))
    return jnp.concatenate(parts, axis=0)


def unpack_rows(stack, slots, size):
    full, rest = divmod(size, LANES)
    parts = [stack[q * slots : (q + 1) * slots] for q in range(full)]
    if rest:
        fold = LANES // rest if LANES % rest == 0 else 1
        base = full * slots
        groups = []
        for g in range(slots // 8):
            line = base + 8 * (g // fold)
            lane = (g % fold) * rest
            groups.append(stack[line : line + 8, lane : lane + rest])
        parts.append(jnp.concatenate(groups, axis=0))
    return jnp.concatenate(parts, axis=1)


def merge_kernel(
    nseq, ntp, slots, npieces, nchunks,
    x_ref, gain_ref, bias_ref, w_ref, mbias_ref, trow_ref, text_ref,
    out_ref,
    stats, xs, tok, wpl, psend, parts, mcol, pick, posend, posbuf, place,
    s_w, r_w, s_z, r_z, s_t, r_t, s_st, r_st, s_p, r_p, s_d, r_d, s_pos, r_pos,
    *buffers,
):
    me, tp = lax.axis_index("seq"), lax.axis_index("tp")
    plane, member = me // GROUP, lax.rem(me, GROUP)
    planes = nseq // GROUP
    owned = planes // ntp
    feats, tokens = x_ref.shape
    rows = tokens // GROUP
    prompt_rows = text_ref.shape[1]
    shard_cols = wpl.shape[1]
    block_cols = shard_cols * GROUP
    chunks = chunks_of(block_cols)
    main, fold = folding(feats, block_cols)
    per = 2 if fold else 1
    wbuf = [buffers[c * per : (c + 1) * per] for c in range(nchunks)]
    send = buffers[npieces : npieces + nchunks]
    got = buffers[npieces + nchunks :]

    def remote(src, dst, send_sem, recv_sem, seq_id, tp_id):
        return pltpu.make_async_remote_copy(
            src_ref=src, dst_ref=dst, send_sem=send_sem, recv_sem=recv_sem,
            device_id=(seq_id, tp_id), device_id_type=MESH,
        )

    barrier = pltpu.get_barrier_semaphore()

    @pl.loop(0, nseq)
    def _(other):
        @pl.when(other != me)
        def _():
            pl.semaphore_signal(barrier, inc=1, device_id=(other, tp), device_id_type=MESH)

    for other_tp in range(ntp):
        @pl.when(other_tp != tp)
        def _():
            for i in range(GROUP):
                pl.semaphore_signal(
                    barrier, inc=1, device_id=(plane * GROUP + i, other_tp), device_id_type=MESH
                )
    pl.semaphore_wait(barrier, nseq - 1 + GROUP * (ntp - 1))

    def weight_copy(i):
        return remote(
            w_ref.at[i], wpl.at[member], s_w.at[i], r_w.at[member], plane * GROUP + i, tp
        )

    def weight_arrival(i):
        return remote(w_ref.at[i], wpl.at[i], s_w.at[i], r_w.at[i], plane * GROUP + i, tp)

    for i in range(GROUP):
        @pl.when(i != member)
        def _():
            weight_copy(i).start()
    wpl[member] = w_ref[member]

    chunk = 256

    @pl.loop(0, tokens // chunk)
    def _(c):
        at = pl.ds(pl.multiple_of(c * chunk, chunk), chunk)
        values = x_ref[:, at].astype(F32)
        mean = jnp.sum(values, axis=0, keepdims=True) / feats
        apart = values - mean
        stats[tp, 0:1, at] = mean
        stats[tp, 1:2, at] = jnp.sum(apart * apart, axis=0, keepdims=True)

    def stats_copy(other_tp, slot):
        return remote(
            stats.at[slot], stats.at[slot], s_st.at[other_tp], r_st.at[slot], me, other_tp
        )

    for other_tp in range(ntp):
        @pl.when(other_tp != tp)
        def _():
            stats_copy(other_tp, tp).start()

    for i in range(GROUP):
        @pl.when(i != member)
        def _():
            weight_arrival(i).wait_recv()
    block = jnp.concatenate([wpl[i].astype(F32) for i in range(GROUP)], axis=0)
    for c, (row0, size) in enumerate(chunks):
        piece = block[row0 : row0 + size]
        wbuf[c][0][plane] = piece[:, :main].astype(BF16)
        if fold:
            part = size // fold
            wbuf[c][1][plane] = jnp.concatenate(
                [piece[q * part : (q + 1) * part, main:] for q in range(fold)], axis=1
            ).astype(BF16)

    def relay(zz, c, up):
        target = (plane + 1 if up else plane - 1) * GROUP + member
        way = 1 if up else 0
        return [
            remote(
                ref.at[zz], ref.at[zz], s_z.at[way, zz, c * per + q], r_z.at[zz, c * per + q],
                target, tp,
            )
            for q, ref in enumerate(wbuf[c])
        ]

    def pass_on(zz, c, act):
        @pl.when((zz <= plane) & (plane + 1 < planes))
        def _():
            for copy in relay(zz, c, True):
                act(copy)

        @pl.when((zz >= plane) & (plane > 0))
        def _():
            for copy in relay(zz, c, False):
                act(copy)

    def take_and_pass(far, c):
        @pl.loop(0, 2)
        def _(side):
            zz = plane + (2 * side - 1) * far

            @pl.when((zz >= 0) & (zz < planes))
            def _():
                for copy in relay(zz, c, True):
                    copy.wait_recv()
                pass_on(zz, c, lambda copy: copy.start())

    for c in range(nchunks):
        pass_on(plane, c, lambda copy: copy.start())

    for other_tp in range(ntp):
        @pl.when(other_tp != tp)
        def _():
            stats_copy(other_tp, other_tp).wait_recv()
    columns = jnp.concatenate(
        [ref[...].astype(F32) for ref in (gain_ref, bias_ref, mbias_ref)]
        + [jnp.zeros((5, feats), F32)],
        axis=0,
    ).T
    gain, bias = columns[:, 0:1], columns[:, 1:2]
    mcol[...] = jnp.broadcast_to(columns[:, 2:3], (feats, LANES))
    wide = GROUP * LANES
    from_tok = lax.broadcasted_iota(jnp.int32, (wide, wide), 0)
    to_tok = lax.broadcasted_iota(jnp.int32, (wide, wide), 1)
    sorter = (from_tok == GROUP * (to_tok % LANES) + to_tok // LANES).astype(F32).astype(BF16)
    for c in range(tokens // wide):
        at = slice(c * wide, (c + 1) * wide)
        mean = sum(stats[q, 0:1, at] for q in range(ntp)) / ntp
        square = sum(
            stats[q, 1:2, at] + feats * (stats[q, 0:1, at] - mean) ** 2 for q in range(ntp)
        )
        scale = lax.rsqrt(square / (feats * ntp) + 1e-06)
        normed = (
            (x_ref[:, at].astype(F32) - mean) * scale * gain + bias
        ).astype(BF16)
        by_patch = jnp.dot(normed, sorter, preferred_element_type=F32).astype(BF16)
        for i in range(GROUP):
            xs[i, :, c * LANES : (c + 1) * LANES] = by_patch[:, i * LANES : (i + 1) * LANES]

    def token_copy(i, slot, sem):
        return remote(xs.at[i], tok.at[slot], s_t.at[i], r_t.at[sem], plane * GROUP + i, tp)

    for i in range(GROUP):
        @pl.when(i != member)
        def _():
            token_copy(i, member, member).start()
    tok[member] = xs[member]

    trow = trow_ref[...]
    tcol = jnp.broadcast_to(trow.astype(F32), (8, rows)).T[:, 0:1].astype(jnp.int32)
    dest_row = trow // prompt_rows
    dest_col = tcol // prompt_rows
    first = lax.broadcasted_iota(jnp.int32, (rows, rows), 0)
    second = lax.broadcasted_iota(jnp.int32, (rows, rows), 1)
    same = dest_col == dest_row
    order_row = jnp.sum((same & (first < second)).astype(F32), axis=0, keepdims=True)
    order_col = jnp.sum((same & (second < first)).astype(F32), axis=1, keepdims=True)
    slot_row = dest_row * slots + order_row.astype(jnp.int32)
    slot_col = dest_col * slots + order_col.astype(jnp.int32)
    local_col = (tcol - dest_col * prompt_rows + 1).astype(F32)

    @pl.loop(0, planes)
    def _(to):
        size = GROUP * slots
        slot_at = to * size + lax.broadcasted_iota(jnp.int32, (size, rows), 0)
        pick[to] = (slot_at == slot_row).astype(F32).astype(BF16)

    def pos_copy(other, slot):
        return remote(
            posend.at[other], posbuf.at[slot], s_pos.at[other], r_pos.at[slot], other, tp
        )

    @pl.loop(0, nseq)
    def _(other):
        base = other * slots
        lane = lax.broadcasted_iota(jnp.int32, (rows, LANES), 1)
        held = jnp.where((slot_col == base + lane) & (lane < slots), local_col, 0.0)
        posend[other] = jnp.broadcast_to(jnp.sum(held, axis=0, keepdims=True), (8, LANES))

        @pl.when(other != me)
        def _():
            pos_copy(other, me).start()

        @pl.when(other == me)
        def _():
            posbuf[me] = posend[me]

    def part_copy(zz, c, i):
        home = zz // owned
        at = pl.ds(*chunks[c])
        return remote(
            psend.at[zz, i, at],
            parts.at[zz - home * owned, member * ntp + tp, at],
            s_p.at[zz, c, i],
            r_p.at[zz - home * owned, c, member * ntp + tp],
            plane * GROUP + i,
            home,
        )

    def here(zz, i):
        return (zz // owned == tp) & (i == member)

    def use_chunk(zz, c):
        at = pl.ds(*chunks[c])
        weight = wbuf[c][0][zz]
        if fold:
            lanes = LANES // fold
            rest = wbuf[c][1][zz]
            rest = jnp.concatenate(
                [rest[:, q * lanes : (q + 1) * lanes] for q in range(fold)], axis=0
            )
            weight = jnp.concatenate([weight, rest], axis=1)
        for i in range(GROUP):
            psend[zz, i, at] = contract(weight, tok[i], 1, 0).astype(BF16)

            @pl.when(jnp.logical_not(here(zz, i)))
            def _():
                part_copy(zz, c, i).start()

            @pl.when(here(zz, i))
            def _():
                parts[zz - tp * owned, member * ntp + tp, at] = psend[zz, i, at]

    def row_copy(b, c, other, slot):
        return remote(
            send[c].at[b, other], got[c].at[b, slot],
            s_d.at[b, c, other], r_d.at[b, c, slot], other, tp,
        )

    def place_chunk(zz, c):
        b = zz - tp * owned
        row0, size = chunks[c]
        at = pl.ds(row0, size)
        total = jnp.zeros((size, rows), F32)
        for i in range(GROUP):
            for q in range(ntp):
                @pl.when((i != member) | (q != tp))
                def _():
                    remote(
                        psend.at[0, 0, at], parts.at[b, i * ntp + q, at],
                        s_p.at[0, c, 0], r_p.at[b, c, i * ntp + q], me, q,
                    ).wait_recv()
                total = total + parts[b, i * ntp + q, at].astype(F32)
        shift = mcol[pl.ds(pl.multiple_of(b * block_cols + row0, 8), size), :][:, 0:1]
        merged = (total + shift).astype(BF16)

        @pl.loop(0, planes)
        def _(step):
            to = lax.rem(plane + planes // 2 + step, planes)
            picked = contract(pick[to], merged, 1, 1)
            for i in range(GROUP):
                other = to * GROUP + i
                send[c][b, other] = pack_rows(
                    picked[i * slots : (i + 1) * slots], slots, size
                ).astype(BF16)

                @pl.when(other != me)
                def _():
                    row_copy(b, c, other, me).start()

                @pl.when(other == me)
                def _():
                    got[c][b, me] = send[c][b, me]

    def both_sides(far, act):
        @pl.loop(0, 2)
        def _(side):
            zz = plane + (2 * side - 1) * far

            @pl.when((zz >= 0) & (zz < planes) & ((far > 0) | (side == 0)))
            def _():
                act(zz)

    def place_both(far, c):
        def act(zz):
            @pl.when(zz // owned == tp)
            def _():
                place_chunk(zz, c)

        both_sides(far, act)

    for c in range(nchunks):
        take_and_pass(1, c)
    for i in range(GROUP):
        @pl.when(i != member)
        def _():
            token_copy(i, i, i).wait_recv()

    @pl.loop(0, planes)
    def _(far):
        for c in range(nchunks):
            @pl.when(far > 1)
            def _():
                take_and_pass(far, c)
            both_sides(far, lambda zz: use_chunk(zz, c))
            if c:
                place_both(far, c - 1)
            else:
                @pl.when(far > 0)
                def _():
                    place_both(far - 1, nchunks - 1)

    diagonal = lax.broadcasted_iota(jnp.int32, (slots, LANES), 0) == lax.broadcasted_iota(
        jnp.int32, (slots, LANES), 1
    )
    position = (
        lax.broadcasted_iota(jnp.int32, (GROUP * slots, prompt_rows), 1).astype(F32) + 1.0
    )

    def spots(source, hits):
        lines = []
        for i in range(GROUP):
            other = source * GROUP + i

            @pl.when(other != me)
            def _():
                pos_copy(other, other).wait_recv()
            line = posbuf[other][0:1]
            lines.append(jnp.sum(jnp.where(diagonal, line, 0.0), axis=1, keepdims=True))
        spot = (jnp.concatenate(lines, axis=0) == position).astype(F32)
        place[source] = spot.astype(BF16)
        return hits + jnp.sum(spot, axis=0, keepdims=True)

    hits = lax.fori_loop(0, planes, spots, jnp.zeros((1, prompt_rows), F32))
    place_both(planes - 1, nchunks - 1)

    for b in range(owned):
        for c, (row0, size) in enumerate(chunks):
            @pl.loop(0, nseq)
            def _(other):
                @pl.when(other != me)
                def _():
                    row_copy(b, c, other, other).wait_recv()
            arrived = jnp.concatenate(
                [unpack_rows(got[c][b, s].astype(F32), slots, size) for s in range(nseq)], axis=0
            ).astype(BF16)
            image = contract(arrived, place[...].reshape(nseq * slots, prompt_rows), 0, 0)
            at = slice(b * block_cols + row0, b * block_cols + row0 + size)
            out_ref[at, :] = jnp.where(hits > 0.5, image.astype(BF16), text_ref[at, :])

    for i in range(GROUP):
        @pl.when(i != member)
        def _():
            weight_copy(i).wait_send()
            token_copy(i, member, member).wait_send()
    for other_tp in range(ntp):
        @pl.when(other_tp != tp)
        def _():
            stats_copy(other_tp, tp).wait_send()

    @pl.loop(0, planes)
    def _(zz):
        for c in range(nchunks):
            pass_on(zz, c, lambda copy: copy.wait_send())
            for i in range(GROUP):
                @pl.when(jnp.logical_not(here(zz, i)))
                def _():
                    part_copy(zz, c, i).wait_send()

    @pl.loop(0, nseq)
    def _(other):
        @pl.when(other != me)
        def _():
            pos_copy(other, me).wait_send()
            for b in range(owned):
                for c in range(nchunks):
                    row_copy(b, c, other, me).wait_send()


def shards(patches, ln_gain, ln_bias, merge_weight, merge_bias, targets, text_embed):
    nseq, ntp = lax.axis_size("seq"), lax.axis_size("tp")
    feats, tokens = patches.shape
    rows = tokens // GROUP
    shard_cols = merge_weight.shape[2]
    planes = nseq // GROUP
    owned = planes // ntp
    block_cols = GROUP * shard_cols
    prompt_rows = text_embed.shape[1]
    slots = round_up(5 * rows // (2 * nseq), 8)
    chunks = chunks_of(block_cols)
    main, fold = folding(feats, block_cols)
    pieces = []
    for _, size in chunks:
        pieces.append(pltpu.VMEM((planes, size, main), BF16))
        if fold:
            pieces.append(pltpu.VMEM((planes, size // fold, LANES), BF16))
    payloads = [
        pltpu.VMEM((owned, nseq, payload_rows(slots, size), LANES), BF16)
        for _, size in chunks
    ]
    dma = pltpu.SemaphoreType.DMA
    count = len(chunks)
    return pl.pallas_call(
        functools.partial(merge_kernel, nseq, ntp, slots, len(pieces), count),
        out_shape=jax.ShapeDtypeStruct(text_embed.shape, text_embed.dtype),
        in_specs=[pl.BlockSpec(memory_space=pltpu.VMEM)] * 7,
        out_specs=pl.BlockSpec(memory_space=pltpu.VMEM),
        scratch_shapes=[
            pltpu.VMEM((ntp, 2, tokens), F32),
            pltpu.VMEM((GROUP, feats, rows), BF16),
            pltpu.VMEM((GROUP, feats, rows), BF16),
            pltpu.VMEM((GROUP, shard_cols, feats), BF16),
            pltpu.VMEM((planes, GROUP, block_cols, rows), BF16),
            pltpu.VMEM((owned, GROUP * ntp, block_cols, rows), BF16),
            pltpu.VMEM((feats, LANES), F32),
            pltpu.VMEM((planes, GROUP * slots, rows), BF16),
            pltpu.VMEM((nseq, 8, LANES), F32),
            pltpu.VMEM((nseq, 8, LANES), F32),
            pltpu.VMEM((planes, GROUP * slots, prompt_rows), BF16),
            dma((GROUP,)), dma((GROUP,)),
            dma((2, planes, len(pieces))), dma((planes, len(pieces))),
            dma((GROUP,)), dma((GROUP,)),
            dma((ntp,)), dma((ntp,)),
            dma((planes, count, GROUP)), dma((owned, count, GROUP * ntp)),
            dma((owned, count, nseq)), dma((owned, count, nseq)),
            dma((nseq,)), dma((nseq,)),
        ] + pieces + payloads + payloads,
        compiler_params=pltpu.CompilerParams(
            collective_id=0, has_side_effects=True, vmem_limit_bytes=56 * 2**20
        ),
    )(
        patches,
        ln_gain[None, :],
        ln_bias[None, :],
        jnp.swapaxes(merge_weight, 1, 2),
        merge_bias[None, :],
        targets[None, :],
        text_embed,
    )


def solution(mesh):
    in_specs = (
        P("tp", "seq"),
        P("tp"),
        P("tp"),
        P(None, "tp", "seq"),
        P("tp"),
        P("seq"),
        P("tp", "seq"),
    )
    out_specs = P("tp", "seq")
    return jax.shard_map(shards, mesh=mesh, in_specs=in_specs, out_specs=out_specs, check_vma=False)
```

time: 126 us -> 115 us (0.913)
  Pallas kernels: 116 us -> 109 us
  local copies, waits for them, and re-layouts: 9.62 us -> 5.77 us
    pallas_call x1, Pallas kernels: 116 us -> 109 us  [shards(): pl.pallas_call(functools.partial(merge_kernel, nseq, ntp, slots, len(piec...]
    broadcast_in_dim x4 -> x3, local copies, waits for them, and re-layouts: 6.39 us -> 3.8 us  [the longest x1 1.27 us: shards(): ln_bias[None, :]]
    unnamed x4 -> x1, local copies, waits for them, and re-layouts: 3.23 us -> 1.98 us
where the time goes in v3:
time: 115 us
  Pallas kernels  109 us (95%)
  local copies, waits for them, and re-layouts  5.77 us (5%)
    pallas_call x1, Pallas kernels, shards(): pl.pallas_call(functools.partial(merge_kernel, nseq, ntp, slots, len(piec...  109 us

profile of v3, /device:TPU:0, one launch (start us, length us, event | category | flops | bytes accessed | tf_op | source)
XLA Modules:
  0.0 114.7 jit_solution(1767315111825893261)
XLA Ops:
  0.0 1.3 %broadcast_in_dim.12.gain_ref = bf16[1,832]{1,0:T(2,128)(2,1)} reshape(bf16[832]{0:T(1024)(128)(2,1)} %param.8) | data formatting | bytes 3328 | tf_op jit(solution)/shard_map/broadcast_in_dim | solution.py:531
  1.3 1.3 %broadcast_in_dim.13.bias_ref = bf16[1,832]{1,0:T(2,128)(2,1)} reshape(bf16[832]{0:T(1024)(128)(2,1)} %param.9) | data formatting | bytes 3328 | tf_op jit(solution)/shard_map/broadcast_in_dim | solution.py:532
  2.5 1.3 %broadcast_in_dim.14.mbias_ref = bf16[1,832]{1,0:T(2,128)(2,1)} reshape(bf16[832]{0:T(1024)(128)(2,1)} %param.11) | data formatting | bytes 3328 | tf_op jit(solution)/shard_map/broadcast_in_dim | solution.py:534
  3.8 108.9 %shard_map.73 = bf16[832,384]{1,0:T(8,128)(2,1)} custom-call(bf16[832,1024]{1,0:T(8,128)(2,1)} %x_ref.1, bf16[1,832]{1,0:T(2,128)(2,1)} %broadcast_in_dim.12.gain_ref, bf16[1,832]{1,0:T(2,128)(2,1)} %broadcast_in_dim.13.bias_ref, bf16[4,104,832]{2,1,0:T(8,128)(2,1)} %bitcast.2, bf16[1,832]{1,0:T(2,128)(2,1)} %broadcast_in_dim.14.mbias_ref, ...), custom_call_target="tpu_custom_call" | custom-call | tf_op jit(solution)/shard_map/pallas_call | solution.py:501
  112.7 2.0 %copy.9 = bf16[832,384]{1,0:T(8,128)(2,1)} copy(bf16[832,384]{1,0:T(8,128)(2,1)} %shard_map.73) | data formatting | bytes 1277952

commit v4 on v3

--- a/solution.py
+++ b/solution.py
@@ -86,10 +86,10 @@
 
 def merge_kernel(
     nseq, ntp, slots, npieces, nchunks,
-    x_ref, gain_ref, bias_ref, w_ref, mbias_ref, trow_ref, text_ref,
+    x_ref, vec_ref, w_ref, trow_ref, text_ref,
     out_ref,
-    stats, xs, tok, wpl, psend, parts, mcol, pick, posend, posbuf, place,
-    s_w, r_w, s_z, r_z, s_t, r_t, s_st, r_st, s_p, r_p, s_d, r_d, s_pos, r_pos,
+    stats, xs, tok, wpl, psend, cores, summed, parts, mcol, pick, posend, posbuf, place,
+    s_w, r_w, s_z, r_z, s_t, r_t, s_st, r_st, s_c, r_c, s_p, r_p, s_d, r_d, s_pos, r_pos,
     *buffers,
 ):
     me, tp = lax.axis_index("seq"), lax.axis_index("tp")
@@ -221,8 +221,7 @@
         def _():
             stats_copy(other_tp, other_tp).wait_recv()
     columns = jnp.concatenate(
-        [ref[...].astype(F32) for ref in (gain_ref, bias_ref, mbias_ref)]
-        + [jnp.zeros((5, feats), F32)],
+        [vec_ref[:, q * feats : (q + 1) * feats] for q in range(3)] + [jnp.zeros((5, feats), F32)],
         axis=0,
     ).T
     gain, bias = columns[:, 0:1], columns[:, 1:2]
@@ -293,20 +292,20 @@
         def _():
             posbuf[me] = posend[me]
 
-    def part_copy(zz, c, i):
+    def core_copy(zz, c):
         home = zz // owned
         at = pl.ds(*chunks[c])
         return remote(
-            psend.at[zz, i, at],
-            parts.at[zz - home * owned, member * ntp + tp, at],
-            s_p.at[zz, c, i],
-            r_p.at[zz - home * owned, c, member * ntp + tp],
-            plane * GROUP + i,
-            home,
-        )
-
-    def here(zz, i):
-        return (zz // owned == tp) & (i == member)
+            psend.at[zz, :, at], cores.at[zz - home * owned, tp, :, at],
+            s_c.at[zz, c], r_c.at[zz - home * owned, c, tp], me, home,
+        )
+
+    def part_copy(b, c, i):
+        at = pl.ds(*chunks[c])
+        return remote(
+            summed.at[b, i, at], parts.at[b, member, at],
+            s_p.at[b, c, i], r_p.at[b, c, member], plane * GROUP + i, tp,
+        )
 
     def use_chunk(zz, c):
         at = pl.ds(*chunks[c])
@@ -321,13 +320,34 @@
         for i in range(GROUP):
             psend[zz, i, at] = contract(weight, tok[i], 1, 0).astype(BF16)
 
-            @pl.when(jnp.logical_not(here(zz, i)))
-            def _():
-                part_copy(zz, c, i).start()
-
-            @pl.when(here(zz, i))
-            def _():
-                parts[zz - tp * owned, member * ntp + tp, at] = psend[zz, i, at]
+        @pl.when(zz // owned != tp)
+        def _():
+            core_copy(zz, c).start()
+
+    def join_chunk(zz, c):
+        b = zz - tp * owned
+        at = pl.ds(*chunks[c])
+        for q in range(ntp):
+            @pl.when(q != tp)
+            def _():
+                remote(
+                    psend.at[zz, :, at], cores.at[b, q, :, at], s_c.at[zz, c], r_c.at[b, c, q], me, q
+                ).wait_recv()
+
+            @pl.when(q == tp)
+            def _():
+                cores[b, q, :, at] = psend[zz, :, at]
+        for i in range(GROUP):
+            total = sum(cores[b, q, i, at].astype(F32) for q in range(ntp))
+            summed[b, i, at] = total.astype(BF16)
+
+            @pl.when(i != member)
+            def _():
+                part_copy(b, c, i).start()
+
+            @pl.when(i == member)
+            def _():
+                parts[b, member, at] = summed[b, i, at]
 
     def row_copy(b, c, other, slot):
         return remote(
@@ -341,14 +361,13 @@
         at = pl.ds(row0, size)
         total = jnp.zeros((size, rows), F32)
         for i in range(GROUP):
-            for q in range(ntp):
-                @pl.when((i != member) | (q != tp))
-                def _():
-                    remote(
-                        psend.at[0, 0, at], parts.at[b, i * ntp + q, at],
-                        s_p.at[0, c, 0], r_p.at[b, c, i * ntp + q], me, q,
-                    ).wait_recv()
-                total = total + parts[b, i * ntp + q, at].astype(F32)
+            @pl.when(i != member)
+            def _():
+                remote(
+                    summed.at[b, i, at], parts.at[b, i, at],
+                    s_p.at[b, c, i], r_p.at[b, c, i], plane * GROUP + i, tp,
+                ).wait_recv()
+            total = total + parts[b, i, at].astype(F32)
         shift = mcol[pl.ds(pl.multiple_of(b * block_cols + row0, 8), size), :][:, 0:1]
         merged = (total + shift).astype(BF16)
 
@@ -379,13 +398,13 @@
             def _():
                 act(zz)
 
-    def place_both(far, c):
-        def act(zz):
+    def owned_sides(far, c, act):
+        def act_owned(zz):
             @pl.when(zz // owned == tp)
             def _():
-                place_chunk(zz, c)
-
-        both_sides(far, act)
+                act(zz, c)
+
+        both_sides(far, act_owned)
 
     for c in range(nchunks):
         take_and_pass(1, c)
@@ -402,11 +421,12 @@
                 take_and_pass(far, c)
             both_sides(far, lambda zz: use_chunk(zz, c))
             if c:
-                place_both(far, c - 1)
+                owned_sides(far, c - 1, place_chunk)
             else:
                 @pl.when(far > 0)
                 def _():
-                    place_both(far - 1, nchunks - 1)
+                    owned_sides(far - 1, nchunks - 1, place_chunk)
+            owned_sides(far, c, join_chunk)
 
     diagonal = lax.broadcasted_iota(jnp.int32, (slots, LANES), 0) == lax.broadcasted_iota(
         jnp.int32, (slots, LANES), 1
@@ -430,7 +450,7 @@
         return hits + jnp.sum(spot, axis=0, keepdims=True)
 
     hits = lax.fori_loop(0, planes, spots, jnp.zeros((1, prompt_rows), F32))
-    place_both(planes - 1, nchunks - 1)
+    owned_sides(planes - 1, nchunks - 1, place_chunk)
 
     for b in range(owned):
         for c, (row0, size) in enumerate(chunks):
@@ -460,10 +480,17 @@
     def _(zz):
         for c in range(nchunks):
             pass_on(zz, c, lambda copy: copy.wait_send())
-            for i in range(GROUP):
-                @pl.when(jnp.logical_not(here(zz, i)))
-                def _():
-                    part_copy(zz, c, i).wait_send()
+
+            @pl.when(zz // owned != tp)
+            def _():
+                core_copy(zz, c).wait_send()
+
+            @pl.when(zz // owned == tp)
+            def _():
+                for i in range(GROUP):
+                    @pl.when(i != member)
+                    def _():
+                        part_copy(zz - tp * owned, c, i).wait_send()
 
     @pl.loop(0, nseq)
     def _(other):
@@ -501,7 +528,7 @@
     return pl.pallas_call(
         functools.partial(merge_kernel, nseq, ntp, slots, len(pieces), count),
         out_shape=jax.ShapeDtypeStruct(text_embed.shape, text_embed.dtype),
-        in_specs=[pl.BlockSpec(memory_space=pltpu.VMEM)] * 7,
+        in_specs=[pl.BlockSpec(memory_space=pltpu.VMEM)] * 5,
         out_specs=pl.BlockSpec(memory_space=pltpu.VMEM),
         scratch_shapes=[
             pltpu.VMEM((ntp, 2, tokens), F32),
@@ -509,7 +536,9 @@
             pltpu.VMEM((GROUP, feats, rows), BF16),
             pltpu.VMEM((GROUP, shard_cols, feats), BF16),
             pltpu.VMEM((planes, GROUP, block_cols, rows), BF16),
-            pltpu.VMEM((owned, GROUP * ntp, block_cols, rows), BF16),
+            pltpu.VMEM((owned, ntp, GROUP, block_cols, rows), BF16),
+            pltpu.VMEM((owned, GROUP, block_cols, rows), BF16),
+            pltpu.VMEM((owned, GROUP, block_cols, rows), BF16),
             pltpu.VMEM((feats, LANES), F32),
             pltpu.VMEM((planes, GROUP * slots, rows), BF16),
             pltpu.VMEM((nseq, 8, LANES), F32),
@@ -519,7 +548,8 @@
             dma((2, planes, len(pieces))), dma((planes, len(pieces))),
             dma((GROUP,)), dma((GROUP,)),
             dma((ntp,)), dma((ntp,)),
-            dma((planes, count, GROUP)), dma((owned, count, GROUP * ntp)),
+            dma((planes, count)), dma((owned, count, ntp)),
+            dma((owned, count, GROUP)), dma((owned, count, GROUP)),
             dma((owned, count, nseq)), dma((owned, count, nseq)),
             dma((nseq,)), dma((nseq,)),
         ] + pieces + payloads + payloads,
@@ -528,10 +558,8 @@
         ),
     )(
         patches,
-        ln_gain[None, :],
-        ln_bias[None, :],
+        jnp.concatenate([v.astype(F32) for v in (ln_gain, ln_bias, merge_bias)])[None, :],
         jnp.swapaxes(merge_weight, 1, 2),
-        merge_bias[None, :],
         targets[None, :],
         text_embed,
     )

time: 115 us -> 112 us (0.974)
  Pallas kernels: 109 us -> 107 us
    broadcast_in_dim x3 -> x1, local copies, waits for them, and re-layouts: 3.8 us -> 0.61 us  [shards(): jnp.concatenate([v.astype(F32) for v in (ln_gain, ln_bias, merge_bias)])]
    concatenate x0 -> x1, local copies, waits for them, and re-layouts: none -> 2.12 us  [shards(): jnp.concatenate([v.astype(F32) for v in (ln_gain, ln_bias, merge_bias)])]
    pallas_call x1, Pallas kernels: 109 us -> 107 us  [shards(): pl.pallas_call(functools.partial(merge_kernel, nseq, ntp, slots, len(piec...]
where the time goes in v4:
time: 112 us
  Pallas kernels  107 us (96%)
  local copies, waits for them, and re-layouts  4.71 us (4%)
    pallas_call x1, Pallas kernels, shards(): pl.pallas_call(functools.partial(merge_kernel, nseq, ntp, slots, len(piec...  107 us

profile of v4, /device:TPU:0, one launch (start us, length us, event | category | flops | bytes accessed | tf_op | source)
XLA Modules:
  0.0 112.0 jit_solution(9604689578956154955)
XLA Ops:
  0.0 2.1 %concatenate.4 = bf16[2496]{0:T(1024)(128)(2,1)S(1)} concatenate(bf16[832]{0:T(1024)(128)(2,1)} %param.8, bf16[832]{0:T(1024)(128)(2,1)} %param.9, bf16[832]{0:T(1024)(128)(2,1)} %param.11), dimensions={0} | concatenate | bytes 9984 | tf_op jit(solution)/shard_map/concatenate | solution.py:561
  2.1 0.6 reshape.vec_ref
  2.7 107.3 %shard_map.73 = bf16[832,384]{1,0:T(8,128)(2,1)} custom-call(bf16[832,1024]{1,0:T(8,128)(2,1)} %x_ref.1, f32[1,2496]{1,0:T(1,128)} %reshape.vec_ref, bf16[4,104,832]{2,1,0:T(8,128)(2,1)} %bitcast.2, s32[1,256]{1,0:T(1,128)} %bitcast.3, bf16[832,384]{1,0:T(8,128)(2,1)} %text_ref.1), custom_call_target="tpu_custom_call" | custom-call | tf_op jit(solution)/shard_map/pallas_call | solution.py:528
  110.1 2.0 %copy.9 = bf16[832,384]{1,0:T(8,128)(2,1)} copy(bf16[832,384]{1,0:T(8,128)(2,1)} %shard_map.73) | data formatting | bytes 1277952

commit v5 on v4

--- a/solution.py
+++ b/solution.py
@@ -253,6 +253,122 @@
             token_copy(i, member, member).start()
     tok[member] = xs[member]
 
+    def core_copy(zz, c):
+        home = zz // owned
+        at = pl.ds(*chunks[c])
+        return remote(
+            psend.at[zz, :, at], cores.at[zz - home * owned, tp, :, at],
+            s_c.at[zz, c], r_c.at[zz - home * owned, c, tp], me, home,
+        )
+
+    def part_copy(b, c, i):
+        at = pl.ds(*chunks[c])
+        return remote(
+            summed.at[b, i, at], parts.at[b, member, at],
+            s_p.at[b, c, i], r_p.at[b, c, member], plane * GROUP + i, tp,
+        )
+
+    def use_chunk(zz, c):
+        at = pl.ds(*chunks[c])
+        weight = wbuf[c][0][zz]
+        if fold:
+            lanes = LANES // fold
+            rest = wbuf[c][1][zz]
+            rest = jnp.concatenate(
+                [rest[:, q * lanes : (q + 1) * lanes] for q in range(fold)], axis=0
+            )
+            weight = jnp.concatenate([weight, rest], axis=1)
+        for i in range(GROUP):
+            psend[zz, i, at] = contract(weight, tok[i], 1, 0).astype(BF16)
+
+        @pl.when(zz // owned != tp)
+        def _():
+            core_copy(zz, c).start()
+
+    def join_chunk(zz, c):
+        b = zz - tp * owned
+        at = pl.ds(*chunks[c])
+        for q in range(ntp):
+            @pl.when(q != tp)
+            def _():
+                remote(
+                    psend.at[zz, :, at], cores.at[b, q, :, at], s_c.at[zz, c], r_c.at[b, c, q], me, q
+                ).wait_recv()
+
+            @pl.when(q == tp)
+            def _():
+                cores[b, q, :, at] = psend[zz, :, at]
+        for i in range(GROUP):
+            total = sum(cores[b, q, i, at].astype(F32) for q in range(ntp))
+            summed[b, i, at] = total.astype(BF16)
+
+            @pl.when(i != member)
+            def _():
+                part_copy(b, c, i).start()
+
+            @pl.when(i == member)
+            def _():
+                parts[b, member, at] = summed[b, i, at]
+
+    def row_copy(b, c, other, slot):
+        return remote(
+            send[c].at[b, other], got[c].at[b, slot],
+            s_d.at[b, c, other], r_d.at[b, c, slot], other, tp,
+        )
+
+    def place_chunk(zz, c):
+        b = zz - tp * owned
+        row0, size = chunks[c]
+        at = pl.ds(row0, size)
+        total = jnp.zeros((size, rows), F32)
+        for i in range(GROUP):
+            @pl.when(i != member)
+            def _():
+                remote(
+                    summed.at[b, i, at], parts.at[b, i, at],
+                    s_p.at[b, c, i], r_p.at[b, c, i], plane * GROUP + i, tp,
+                ).wait_recv()
+            total = total + parts[b, i, at].astype(F32)
+        shift = mcol[pl.ds(pl.multiple_of(b * block_cols + row0, 8), size), :][:, 0:1]
+        merged = (total + shift).T.astype(BF16)
+
+        @pl.loop(0, planes)
+        def _(step):
+            to = lax.rem(plane + planes // 2 + step, planes)
+            picked = contract(pick[to], merged, 1, 0)
+            for i in range(GROUP):
+                other = to * GROUP + i
+                send[c][b, other] = pack_rows(
+                    picked[i * slots : (i + 1) * slots], slots, size
+                ).astype(BF16)
+
+                @pl.when(other != me)
+                def _():
+                    row_copy(b, c, other, me).start()
+
+                @pl.when(other == me)
+                def _():
+                    got[c][b, me] = send[c][b, me]
+
+    def both_sides(far, act):
+        @pl.loop(0, 2)
+        def _(side):
+            zz = plane + (2 * side - 1) * far
+
+            @pl.when((zz >= 0) & (zz < planes) & ((far > 0) | (side == 0)))
+            def _():
+                act(zz)
+
+    def owned_sides(far, c, act):
+        def act_owned(zz):
+            @pl.when(zz // owned == tp)
+            def _():
+                act(zz, c)
+
+        both_sides(far, act_owned)
+
+    take_and_pass(1, 0)
+
     trow = trow_ref[...]
     tcol = jnp.broadcast_to(trow.astype(F32), (8, rows)).T[:, 0:1].astype(jnp.int32)
     dest_row = trow // prompt_rows
@@ -272,6 +388,9 @@
         slot_at = to * size + lax.broadcasted_iota(jnp.int32, (size, rows), 0)
         pick[to] = (slot_at == slot_row).astype(F32).astype(BF16)
 
+    for c in range(1, nchunks):
+        take_and_pass(1, c)
+
     def pos_copy(other, slot):
         return remote(
             posend.at[other], posbuf.at[slot], s_pos.at[other], r_pos.at[slot], other, tp
@@ -292,134 +411,33 @@
         def _():
             posbuf[me] = posend[me]
 
-    def core_copy(zz, c):
-        home = zz // owned
-        at = pl.ds(*chunks[c])
-        return remote(
-            psend.at[zz, :, at], cores.at[zz - home * owned, tp, :, at],
-            s_c.at[zz, c], r_c.at[zz - home * owned, c, tp], me, home,
-        )
-
-    def part_copy(b, c, i):
-        at = pl.ds(*chunks[c])
-        return remote(
-            summed.at[b, i, at], parts.at[b, member, at],
-            s_p.at[b, c, i], r_p.at[b, c, member], plane * GROUP + i, tp,
-        )
-
-    def use_chunk(zz, c):
-        at = pl.ds(*chunks[c])
-        weight = wbuf[c][0][zz]
-        if fold:
-            lanes = LANES // fold
-            rest = wbuf[c][1][zz]
-            rest = jnp.concatenate(
-                [rest[:, q * lanes : (q + 1) * lanes] for q in range(fold)], axis=0
-            )
-            weight = jnp.concatenate([weight, rest], axis=1)
-        for i in range(GROUP):
-            psend[zz, i, at] = contract(weight, tok[i], 1, 0).astype(BF16)
-
-        @pl.when(zz // owned != tp)
-        def _():
-            core_copy(zz, c).start()
-
-    def join_chunk(zz, c):
-        b = zz - tp * owned
-        at = pl.ds(*chunks[c])
-        for q in range(ntp):
-            @pl.when(q != tp)
-            def _():
-                remote(
-                    psend.at[zz, :, at], cores.at[b, q, :, at], s_c.at[zz, c], r_c.at[b, c, q], me, q
-                ).wait_recv()
-
-            @pl.when(q == tp)
-            def _():
-                cores[b, q, :, at] = psend[zz, :, at]
-        for i in range(GROUP):
-            total = sum(cores[b, q, i, at].astype(F32) for q in range(ntp))
-            summed[b, i, at] = total.astype(BF16)
-
-            @pl.when(i != member)
-            def _():
-                part_copy(b, c, i).start()
-
-            @pl.when(i == member)
-            def _():
-                parts[b, member, at] = summed[b, i, at]
-
-    def row_copy(b, c, other, slot):
-        return remote(
-            send[c].at[b, other], got[c].at[b, slot],
-            s_d.at[b, c, other], r_d.at[b, c, slot], other, tp,
-        )
-
-    def place_chunk(zz, c):
-        b = zz - tp * owned
-        row0, size = chunks[c]
-        at = pl.ds(row0, size)
-        total = jnp.zeros((size, rows), F32)
-        for i in range(GROUP):
-            @pl.when(i != member)
-            def _():
-                remote(
-                    summed.at[b, i, at], parts.at[b, i, at],
-                    s_p.at[b, c, i], r_p.at[b, c, i], plane * GROUP + i, tp,
-                ).wait_recv()
-            total = total + parts[b, i, at].astype(F32)
-        shift = mcol[pl.ds(pl.multiple_of(b * block_cols + row0, 8), size), :][:, 0:1]
-        merged = (total + shift).astype(BF16)
-
-        @pl.loop(0, planes)
-        def _(step):
-            to = lax.rem(plane + planes // 2 + step, planes)
-            picked = contract(pick[to], merged, 1, 1)
-            for i in range(GROUP):
-                other = to * GROUP + i
-                send[c][b, other] = pack_rows(
-                    picked[i * slots : (i + 1) * slots], slots, size
-                ).astype(BF16)
-
-                @pl.when(other != me)
-                def _():
-                    row_copy(b, c, other, me).start()
-
-                @pl.when(other == me)
-                def _():
-                    got[c][b, me] = send[c][b, me]
-
-    def both_sides(far, act):
-        @pl.loop(0, 2)
-        def _(side):
-            zz = plane + (2 * side - 1) * far
-
-            @pl.when((zz >= 0) & (zz < planes) & ((far > 0) | (side == 0)))
-            def _():
-                act(zz)
-
-    def owned_sides(far, c, act):
-        def act_owned(zz):
-            @pl.when(zz // owned == tp)
-            def _():
-                act(zz, c)
-
-        both_sides(far, act_owned)
-
-    for c in range(nchunks):
-        take_and_pass(1, c)
+    if planes > 3:
+        take_and_pass(2, 0)
     for i in range(GROUP):
         @pl.when(i != member)
         def _():
             token_copy(i, i, i).wait_recv()
+    for c in range(nchunks):
+        use_chunk(plane, c)
+    if planes > 3:
+        for c in range(1, nchunks):
+            take_and_pass(2, c)
+
+    @pl.loop(3, max(planes - 1, 3))
+    def _(far):
+        for c in range(nchunks):
+            take_and_pass(far, c)
 
     @pl.loop(0, planes)
     def _(far):
         for c in range(nchunks):
-            @pl.when(far > 1)
+            @pl.when((far > 1) & (far == planes - 1))
             def _():
                 take_and_pass(far, c)
-            both_sides(far, lambda zz: use_chunk(zz, c))
+
+            @pl.when(far > 0)
+            def _():
+                both_sides(far, lambda zz: use_chunk(zz, c))
             if c:
                 owned_sides(far, c - 1, place_chunk)
             else:

time: 112 us -> 115 us (1.027)
  Pallas kernels: 107 us -> 110 us
    pallas_call x1, Pallas kernels: 107 us -> 110 us  [shards(): pl.pallas_call(functools.partial(merge_kernel, nseq, ntp, slots, len(piec...]
where the time goes in v5:
time: 115 us; the launch traced here: 114 us
  Pallas kernels  110 us (96%)
  local copies, waits for them, and re-layouts  4.71 us (4%)
    pallas_call x1, Pallas kernels, shards(): pl.pallas_call(functools.partial(merge_kernel, nseq, ntp, slots, len(piec...  110 us

profile of v5, /device:TPU:0, one launch (start us, length us, event | category | flops | bytes accessed | tf_op | source)
XLA Modules:
  0.0 114.3 jit_solution(7913152819849078557)
XLA Ops:
  0.0 2.1 %concatenate.4 = bf16[2496]{0:T(1024)(128)(2,1)S(1)} concatenate(bf16[832]{0:T(1024)(128)(2,1)} %param.8, bf16[832]{0:T(1024)(128)(2,1)} %param.9, bf16[832]{0:T(1024)(128)(2,1)} %param.11), dimensions={0} | concatenate | bytes 9984 | tf_op jit(solution)/shard_map/concatenate | solution.py:579
  2.1 0.6 reshape.vec_ref
  2.7 109.5 %shard_map.73 = bf16[832,384]{1,0:T(8,128)(2,1)} custom-call(bf16[832,1024]{1,0:T(8,128)(2,1)} %x_ref.1, f32[1,2496]{1,0:T(1,128)} %reshape.vec_ref, bf16[4,104,832]{2,1,0:T(8,128)(2,1)} %bitcast.2, s32[1,256]{1,0:T(1,128)} %bitcast.3, bf16[832,384]{1,0:T(8,128)(2,1)} %text_ref.1), custom_call_target="tpu_custom_call" | custom-call | tf_op jit(solution)/shard_map/pallas_call | solution.py:546
  112.3 2.0 %copy.9 = bf16[832,384]{1,0:T(8,128)(2,1)} copy(bf16[832,384]{1,0:T(8,128)(2,1)} %shard_map.73) | data formatting | bytes 1277952

commit v6 on v5

--- a/solution.py
+++ b/solution.py
@@ -25,21 +25,15 @@
     return -(-value // unit) * unit
 
 
-def chunks_of(block_cols):
-    first = (block_cols // LANES + 1) // 2 * LANES
-    if first and first < block_cols and first % 32 == 0 and block_cols % 32 == 0:
-        return [(0, first), (first, block_cols - first)]
-    return [(0, block_cols)]
-
-
-def folding(feats, block_cols):
+def split_columns(feats, shard_cols):
     main = feats // LANES * LANES
     rest = feats - main
-    if main and rest and LANES % rest == 0:
+    if main and rest and LANES % rest == 0 and shard_cols > 64:
         fold = LANES // rest
-        if all(size % (16 * fold) == 0 for _, size in chunks_of(block_cols)):
-            return main, fold
-    return feats, 0
+        sizes = [64, shard_cols - 64]
+        if all(GROUP * size % (16 * fold) == 0 and size % 8 == 0 for size in sizes) and 64 % (16 * fold) == 0:
+            return sizes, main, fold
+    return [shard_cols], feats, 0
 
 
 def payload_rows(slots, size):
@@ -88,7 +82,7 @@
     nseq, ntp, slots, npieces, nchunks,
     x_ref, vec_ref, w_ref, trow_ref, text_ref,
     out_ref,
-    stats, xs, tok, wpl, psend, cores, summed, parts, mcol, pick, posend, posbuf, place,
+    stats, xs, tok, w_low, wpl0, wpl1, psend, cores, summed, parts, mcol, pick, posend, posbuf, place,
     s_w, r_w, s_z, r_z, s_t, r_t, s_st, r_st, s_c, r_c, s_p, r_p, s_d, r_d, s_pos, r_pos,
     *buffers,
 ):
@@ -99,10 +93,12 @@
     feats, tokens = x_ref.shape
     rows = tokens // GROUP
     prompt_rows = text_ref.shape[1]
-    shard_cols = wpl.shape[1]
+    shard_cols = w_ref.shape[1]
     block_cols = shard_cols * GROUP
-    chunks = chunks_of(block_cols)
-    main, fold = folding(feats, block_cols)
+    sizes, main, fold = split_columns(feats, shard_cols)
+    chunks = []
+    for size in sizes:
+        chunks.append((sum(n for _, n in chunks), GROUP * size))
     per = 2 if fold else 1
     wbuf = [buffers[c * per : (c + 1) * per] for c in range(nchunks)]
     send = buffers[npieces : npieces + nchunks]
@@ -131,19 +127,92 @@
                 )
     pl.semaphore_wait(barrier, nseq - 1 + GROUP * (ntp - 1))
 
-    def weight_copy(i):
-        return remote(
-            w_ref.at[i], wpl.at[member], s_w.at[i], r_w.at[member], plane * GROUP + i, tp
-        )
-
-    def weight_arrival(i):
-        return remote(w_ref.at[i], wpl.at[i], s_w.at[i], r_w.at[i], plane * GROUP + i, tp)
-
-    for i in range(GROUP):
-        @pl.when(i != member)
-        def _():
-            weight_copy(i).start()
-    wpl[member] = w_ref[member]
+    first_cols = sizes[0]
+
+    def weight_copy(i, c, slot):
+        if c:
+            src, dst = w_low.at[i], wpl1.at[slot]
+        else:
+            src = w_ref.at[i, pl.ds(0, first_cols)] if nchunks > 1 else w_ref.at[i]
+            dst = wpl0.at[slot]
+        return remote(src, dst, s_w.at[c, i], r_w.at[c, slot], plane * GROUP + i, tp)
+
+    def send_weight(c):
+        for i in range(GROUP):
+            @pl.when(i != member)
+            def _():
+                weight_copy(i, c, member).start()
+
+    def wait_weight(c):
+        for i in range(GROUP):
+            @pl.when(i != member)
+            def _():
+                weight_copy(i, c, i).wait_recv()
+
+    def fold_lanes(rows_in):
+        part = rows_in.shape[0] // fold
+        return jnp.concatenate(
+            [rows_in[q * part : (q + 1) * part, main:] for q in range(fold)], axis=1
+        ).astype(BF16)
+
+    def unfold_lanes(folded):
+        lanes = LANES // fold
+        return jnp.concatenate(
+            [folded[:, q * lanes : (q + 1) * lanes] for q in range(fold)], axis=0
+        )
+
+    def put_first(slot, rows_in):
+        wbuf[0][0][plane, slot] = rows_in[:, :main]
+        if fold:
+            wbuf[0][1][plane, slot] = fold_lanes(rows_in)
+
+    moves = 2 + (nchunks - 1)
+
+    def relay(zz, move, up):
+        target = (plane + 1 if up else plane - 1) * GROUP + member
+        way = 1 if up else 0
+        copies = []
+        for q, ref in enumerate(wbuf[move // 2]):
+            view = (ref.at[zz, 0], ref.at[zz, pl.ds(1, GROUP - 1)], ref.at[zz])[move]
+            copies.append(
+                remote(
+                    view, view, s_z.at[way, zz, move * per + q], r_z.at[zz, move * per + q],
+                    target, tp,
+                )
+            )
+        return copies
+
+    def pass_on(zz, move, act):
+        @pl.when((zz <= plane) & (plane + 1 < planes))
+        def _():
+            for copy in relay(zz, move, True):
+                act(copy)
+
+        @pl.when((zz >= plane) & (plane > 0))
+        def _():
+            for copy in relay(zz, move, False):
+                act(copy)
+
+    def take_and_pass(far, move):
+        @pl.loop(0, 2)
+        def _(side):
+            zz = plane + (2 * side - 1) * far
+
+            @pl.when((zz >= 0) & (zz < planes))
+            def _():
+                for copy in relay(zz, move, True):
+                    copy.wait_recv()
+                pass_on(zz, move, lambda copy: copy.start())
+
+    send_weight(0)
+    put_first(0, w_ref[member][:first_cols])
+    pass_on(plane, 0, lambda copy: copy.start())
+    if nchunks > 1:
+        for i in range(GROUP):
+            w_low[i, 0 : sizes[1]] = w_ref[i, first_cols:]
+            if w_low.shape[1] > sizes[1]:
+                w_low[i, sizes[1] :] = jnp.zeros((w_low.shape[1] - sizes[1], feats), BF16)
+        send_weight(1)
 
     chunk = 256
 
@@ -166,56 +235,10 @@
         def _():
             stats_copy(other_tp, tp).start()
 
-    for i in range(GROUP):
-        @pl.when(i != member)
-        def _():
-            weight_arrival(i).wait_recv()
-    block = jnp.concatenate([wpl[i].astype(F32) for i in range(GROUP)], axis=0)
-    for c, (row0, size) in enumerate(chunks):
-        piece = block[row0 : row0 + size]
-        wbuf[c][0][plane] = piece[:, :main].astype(BF16)
-        if fold:
-            part = size // fold
-            wbuf[c][1][plane] = jnp.concatenate(
-                [piece[q * part : (q + 1) * part, main:] for q in range(fold)], axis=1
-            ).astype(BF16)
-
-    def relay(zz, c, up):
-        target = (plane + 1 if up else plane - 1) * GROUP + member
-        way = 1 if up else 0
-        return [
-            remote(
-                ref.at[zz], ref.at[zz], s_z.at[way, zz, c * per + q], r_z.at[zz, c * per + q],
-                target, tp,
-            )
-            for q, ref in enumerate(wbuf[c])
-        ]
-
-    def pass_on(zz, c, act):
-        @pl.when((zz <= plane) & (plane + 1 < planes))
-        def _():
-            for copy in relay(zz, c, True):
-                act(copy)
-
-        @pl.when((zz >= plane) & (plane > 0))
-        def _():
-            for copy in relay(zz, c, False):
-                act(copy)
-
-    def take_and_pass(far, c):
-        @pl.loop(0, 2)
-        def _(side):
-            zz = plane + (2 * side - 1) * far
-
-            @pl.when((zz >= 0) & (zz < planes))
-            def _():
-                for copy in relay(zz, c, True):
-                    copy.wait_recv()
-                pass_on(zz, c, lambda copy: copy.start())
-
-    for c in range(nchunks):
-        pass_on(plane, c, lambda copy: copy.start())
-
+    wait_weight(0)
+    for r in range(1, GROUP):
+        put_first(r, wpl0[lax.rem(member + r, GROUP)])
+    pass_on(plane, 1, lambda copy: copy.start())
     for other_tp in range(ntp):
         @pl.when(other_tp != tp)
         def _():
@@ -225,7 +248,14 @@
         axis=0,
     ).T
     gain, bias = columns[:, 0:1], columns[:, 1:2]
-    mcol[...] = jnp.broadcast_to(columns[:, 2:3], (feats, LANES))
+    for b in range(owned):
+        for c, (row0, size) in enumerate(chunks):
+            for i in range(GROUP):
+                come = b * block_cols + i * shard_cols + sum(sizes[:c])
+                go = b * block_cols + row0 + i * sizes[c]
+                mcol[go : go + sizes[c]] = jnp.broadcast_to(
+                    columns[come : come + sizes[c], 2:3], (sizes[c], LANES)
+                )
     wide = GROUP * LANES
     from_tok = lax.broadcasted_iota(jnp.int32, (wide, wide), 0)
     to_tok = lax.broadcasted_iota(jnp.int32, (wide, wide), 1)
@@ -253,6 +283,16 @@
             token_copy(i, member, member).start()
     tok[member] = xs[member]
 
+    if nchunks > 1:
+        wait_weight(1)
+        wpl1[member] = w_low[member]
+        low = jnp.concatenate(
+            [wpl1[i].astype(F32)[: sizes[1]] for i in range(GROUP)], axis=0
+        )
+        wbuf[1][0][plane] = low[:, :main].astype(BF16)
+        wbuf[1][1][plane] = fold_lanes(low)
+        pass_on(plane, 2, lambda copy: copy.start())
+
     def core_copy(zz, c):
         home = zz // owned
         at = pl.ds(*chunks[c])
@@ -270,14 +310,17 @@
 
     def use_chunk(zz, c):
         at = pl.ds(*chunks[c])
-        weight = wbuf[c][0][zz]
-        if fold:
-            lanes = LANES // fold
-            rest = wbuf[c][1][zz]
-            rest = jnp.concatenate(
-                [rest[:, q * lanes : (q + 1) * lanes] for q in range(fold)], axis=0
-            )
-            weight = jnp.concatenate([weight, rest], axis=1)
+        if c:
+            weight = jnp.concatenate([wbuf[1][0][zz], unfold_lanes(wbuf[1][1][zz])], axis=1)
+        else:
+            members = []
+            for i in range(GROUP):
+                slot = lax.rem(i - member + GROUP, GROUP)
+                piece = wbuf[0][0][zz, slot]
+                if fold:
+                    piece = jnp.concatenate([piece, unfold_lanes(wbuf[0][1][zz, slot])], axis=1)
+                members.append(piece if fold else piece.astype(F32))
+            weight = jnp.concatenate(members, axis=0).astype(BF16)
         for i in range(GROUP):
             psend[zz, i, at] = contract(weight, tok[i], 1, 0).astype(BF16)
 
@@ -368,6 +411,7 @@
         both_sides(far, act_owned)
 
     take_and_pass(1, 0)
+    take_and_pass(1, 1)
 
     trow = trow_ref[...]
     tcol = jnp.broadcast_to(trow.astype(F32), (8, rows)).T[:, 0:1].astype(jnp.int32)
@@ -388,8 +432,8 @@
         slot_at = to * size + lax.broadcasted_iota(jnp.int32, (size, rows), 0)
         pick[to] = (slot_at == slot_row).astype(F32).astype(BF16)
 
-    for c in range(1, nchunks):
-        take_and_pass(1, c)
+    if moves > 2:
+        take_and_pass(1, 2)
 
     def pos_copy(other, slot):
         return remote(
@@ -411,33 +455,19 @@
         def _():
             posbuf[me] = posend[me]
 
-    if planes > 3:
-        take_and_pass(2, 0)
     for i in range(GROUP):
         @pl.when(i != member)
         def _():
             token_copy(i, i, i).wait_recv()
-    for c in range(nchunks):
-        use_chunk(plane, c)
-    if planes > 3:
-        for c in range(1, nchunks):
-            take_and_pass(2, c)
-
-    @pl.loop(3, max(planes - 1, 3))
-    def _(far):
-        for c in range(nchunks):
-            take_and_pass(far, c)
 
     @pl.loop(0, planes)
     def _(far):
         for c in range(nchunks):
-            @pl.when((far > 1) & (far == planes - 1))
-            def _():
-                take_and_pass(far, c)
-
-            @pl.when(far > 0)
-            def _():
-                both_sides(far, lambda zz: use_chunk(zz, c))
+            @pl.when(far > 1)
+            def _():
+                for move in (2,) if c else (0, 1):
+                    take_and_pass(far, move)
+            both_sides(far, lambda zz: use_chunk(zz, c))
             if c:
                 owned_sides(far, c - 1, place_chunk)
             else:
@@ -471,6 +501,7 @@
     owned_sides(planes - 1, nchunks - 1, place_chunk)
 
     for b in range(owned):
+        images = []
         for c, (row0, size) in enumerate(chunks):
             @pl.loop(0, nseq)
             def _(other):
@@ -480,14 +511,25 @@
             arrived = jnp.concatenate(
                 [unpack_rows(got[c][b, s].astype(F32), slots, size) for s in range(nseq)], axis=0
             ).astype(BF16)
-            image = contract(arrived, place[...].reshape(nseq * slots, prompt_rows), 0, 0)
-            at = slice(b * block_cols + row0, b * block_cols + row0 + size)
-            out_ref[at, :] = jnp.where(hits > 0.5, image.astype(BF16), text_ref[at, :])
+            images.append(
+                contract(arrived, place[...].reshape(nseq * slots, prompt_rows), 0, 0)
+            )
+        image = jnp.concatenate(
+            [
+                images[c][i * sizes[c] : (i + 1) * sizes[c]]
+                for i in range(GROUP)
+                for c in range(nchunks)
+            ],
+            axis=0,
+        )
+        at = slice(b * block_cols, (b + 1) * block_cols)
+        out_ref[at, :] = jnp.where(hits > 0.5, image.astype(BF16), text_ref[at, :])
 
     for i in range(GROUP):
         @pl.when(i != member)
         def _():
-            weight_copy(i).wait_send()
+            for c in range(nchunks):
+                weight_copy(i, c, member).wait_send()
             token_copy(i, member, member).wait_send()
     for other_tp in range(ntp):
         @pl.when(other_tp != tp)
@@ -496,8 +538,9 @@
 
     @pl.loop(0, planes)
     def _(zz):
+        for move in range(moves):
+            pass_on(zz, move, lambda copy: copy.wait_send())
         for c in range(nchunks):
-            pass_on(zz, c, lambda copy: copy.wait_send())
 
             @pl.when(zz // owned != tp)
             def _():
@@ -530,13 +573,16 @@
     block_cols = GROUP * shard_cols
     prompt_rows = text_embed.shape[1]
     slots = round_up(5 * rows // (2 * nseq), 8)
-    chunks = chunks_of(block_cols)
-    main, fold = folding(feats, block_cols)
-    pieces = []
-    for _, size in chunks:
-        pieces.append(pltpu.VMEM((planes, size, main), BF16))
-        if fold:
-            pieces.append(pltpu.VMEM((planes, size // fold, LANES), BF16))
+    sizes, main, fold = split_columns(feats, shard_cols)
+    chunks = [(0, GROUP * size) for size in sizes]
+    low_rows = round_up(sizes[-1], 16)
+    pieces = [pltpu.VMEM((planes, GROUP, sizes[0], main), BF16)]
+    if fold:
+        pieces += [
+            pltpu.VMEM((planes, GROUP, sizes[0] // fold, LANES), BF16),
+            pltpu.VMEM((planes, GROUP * sizes[1], main), BF16),
+            pltpu.VMEM((planes, GROUP * sizes[1] // fold, LANES), BF16),
+        ]
     payloads = [
         pltpu.VMEM((owned, nseq, payload_rows(slots, size), LANES), BF16)
         for _, size in chunks
@@ -552,7 +598,9 @@
             pltpu.VMEM((ntp, 2, tokens), F32),
             pltpu.VMEM((GROUP, feats, rows), BF16),
             pltpu.VMEM((GROUP, feats, rows), BF16),
-            pltpu.VMEM((GROUP, shard_cols, feats), BF16),
+            pltpu.VMEM((GROUP, low_rows, feats), BF16),
+            pltpu.VMEM((GROUP, sizes[0], feats), BF16),
+            pltpu.VMEM((GROUP, low_rows, feats), BF16),
             pltpu.VMEM((planes, GROUP, block_cols, rows), BF16),
             pltpu.VMEM((owned, ntp, GROUP, block_cols, rows), BF16),
             pltpu.VMEM((owned, GROUP, block_cols, rows), BF16),
@@ -562,8 +610,8 @@
             pltpu.VMEM((nseq, 8, LANES), F32),
             pltpu.VMEM((nseq, 8, LANES), F32),
             pltpu.VMEM((planes, GROUP * slots, prompt_rows), BF16),
-            dma((GROUP,)), dma((GROUP,)),
-            dma((2, planes, len(pieces))), dma((planes, len(pieces))),
+            dma((2, GROUP)), dma((2, GROUP)),
+            dma((2, planes, 6)), dma((planes, 6)),
             dma((GROUP,)), dma((GROUP,)),
             dma((ntp,)), dma((ntp,)),
             dma((planes, count)), dma((owned, count, ntp)),

time: 115 us -> 110 us (0.957)
  Pallas kernels: 110 us -> 105 us
    pallas_call x1, Pallas kernels: 110 us -> 105 us  [shards(): pl.pallas_call(functools.partial(merge_kernel, nseq, ntp, slots, len(piec...]
where the time goes in v6:
time: 110 us
  Pallas kernels  105 us (95%)
  local copies, waits for them, and re-layouts  4.71 us (4%)
    pallas_call x1, Pallas kernels, shards(): pl.pallas_call(functools.partial(merge_kernel, nseq, ntp, slots, len(piec...  105 us

profile of v6, /device:TPU:0, one launch (start us, length us, event | category | flops | bytes accessed | tf_op | source)
XLA Modules:
  0.0 110.2 jit_solution(14880908318792153751)
XLA Ops:
  0.0 2.1 %concatenate.4 = bf16[2496]{0:T(1024)(128)(2,1)S(1)} concatenate(bf16[832]{0:T(1024)(128)(2,1)} %param.8, bf16[832]{0:T(1024)(128)(2,1)} %param.9, bf16[832]{0:T(1024)(128)(2,1)} %param.11), dimensions={0} | concatenate | bytes 9984 | tf_op jit(solution)/shard_map/concatenate | solution.py:627
  2.1 0.6 reshape.vec_ref
  2.7 105.4 %shard_map.73 = bf16[832,384]{1,0:T(8,128)(2,1)} custom-call(bf16[832,1024]{1,0:T(8,128)(2,1)} %x_ref.1, f32[1,2496]{1,0:T(1,128)} %reshape.vec_ref, bf16[4,104,832]{2,1,0:T(8,128)(2,1)} %bitcast.2, s32[1,256]{1,0:T(1,128)} %bitcast.3, bf16[832,384]{1,0:T(8,128)(2,1)} %text_ref.1), custom_call_target="tpu_custom_call" | custom-call | tf_op jit(solution)/shard_map/pallas_call | solution.py:592
  108.2 2.0 %copy.9 = bf16[832,384]{1,0:T(8,128)(2,1)} copy(bf16[832,384]{1,0:T(8,128)(2,1)} %shard_map.73) | data formatting | bytes 1277952

commit v7 on v6

--- a/solution.py
+++ b/solution.py
@@ -80,7 +80,7 @@
 
 def merge_kernel(
     nseq, ntp, slots, npieces, nchunks,
-    x_ref, vec_ref, w_ref, trow_ref, text_ref,
+    x_ref, gain_ref, bias_ref, mbias_ref, w_ref, trow_ref, text_ref,
     out_ref,
     stats, xs, tok, w_low, wpl0, wpl1, psend, cores, summed, parts, mcol, pick, posend, posbuf, place,
     s_w, r_w, s_z, r_z, s_t, r_t, s_st, r_st, s_c, r_c, s_p, r_p, s_d, r_d, s_pos, r_pos,
@@ -244,7 +244,8 @@
         def _():
             stats_copy(other_tp, other_tp).wait_recv()
     columns = jnp.concatenate(
-        [vec_ref[:, q * feats : (q + 1) * feats] for q in range(3)] + [jnp.zeros((5, feats), F32)],
+        [ref[...].astype(F32).reshape(1, feats) for ref in (gain_ref, bias_ref, mbias_ref)]
+        + [jnp.zeros((5, feats), F32)],
         axis=0,
     ).T
     gain, bias = columns[:, 0:1], columns[:, 1:2]
@@ -468,13 +469,13 @@
                 for move in (2,) if c else (0, 1):
                     take_and_pass(far, move)
             both_sides(far, lambda zz: use_chunk(zz, c))
+            owned_sides(far, c, join_chunk)
             if c:
                 owned_sides(far, c - 1, place_chunk)
             else:
                 @pl.when(far > 0)
                 def _():
                     owned_sides(far - 1, nchunks - 1, place_chunk)
-            owned_sides(far, c, join_chunk)
 
     diagonal = lax.broadcasted_iota(jnp.int32, (slots, LANES), 0) == lax.broadcasted_iota(
         jnp.int32, (slots, LANES), 1
@@ -500,7 +501,9 @@
     hits = lax.fori_loop(0, planes, spots, jnp.zeros((1, prompt_rows), F32))
     owned_sides(planes - 1, nchunks - 1, place_chunk)
 
-    for b in range(owned):
+    @pl.loop(0, owned)
+    def _(turn):
+        b = jnp.where(2 * tp < ntp, owned - 1 - turn, turn)
         images = []
         for c, (row0, size) in enumerate(chunks):
             @pl.loop(0, nseq)
@@ -522,7 +525,7 @@
             ],
             axis=0,
         )
-        at = slice(b * block_cols, (b + 1) * block_cols)
+        at = pl.ds(pl.multiple_of(b * block_cols, 8), block_cols)
         out_ref[at, :] = jnp.where(hits > 0.5, image.astype(BF16), text_ref[at, :])
 
     for i in range(GROUP):
@@ -592,7 +595,7 @@
     return pl.pallas_call(
         functools.partial(merge_kernel, nseq, ntp, slots, len(pieces), count),
         out_shape=jax.ShapeDtypeStruct(text_embed.shape, text_embed.dtype),
-        in_specs=[pl.BlockSpec(memory_space=pltpu.VMEM)] * 5,
+        in_specs=[pl.BlockSpec(memory_space=pltpu.VMEM)] * 7,
         out_specs=pl.BlockSpec(memory_space=pltpu.VMEM),
         scratch_shapes=[
             pltpu.VMEM((ntp, 2, tokens), F32),
@@ -624,7 +627,9 @@
         ),
     )(
         patches,
-        jnp.concatenate([v.astype(F32) for v in (ln_gain, ln_bias, merge_bias)])[None, :],
+        ln_gain,
+        ln_bias,
+        merge_bias,
         jnp.swapaxes(merge_weight, 1, 2),
         targets[None, :],
         text_embed,

time: 110 us -> 103 us (0.936)
  Pallas kernels: 105 us -> 101 us
  local copies, waits for them, and re-layouts: 4.71 us -> 1.98 us
    pallas_call x1, Pallas kernels: 105 us -> 101 us  [shards(): pl.pallas_call(functools.partial(merge_kernel, nseq, ntp, slots, len(piec...]
    concatenate x1 -> x0, local copies, waits for them, and re-layouts: 2.12 us -> none  [shards(): jnp.concatenate([v.astype(F32) for v in (ln_gain, ln_bias, merge_bias)])]
where the time goes in v7:
time: 103 us
  Pallas kernels  101 us (98%)
  local copies, waits for them, and re-layouts  1.98 us (2%)
    pallas_call x1, Pallas kernels, shards(): pl.pallas_call(functools.partial(merge_kernel, nseq, ntp, slots, len(piec...  101 us

profile of v7, /device:TPU:0, one launch (start us, length us, event | category | flops | bytes accessed | tf_op | source)
XLA Modules:
  0.0 103.0 jit_solution(7270189859496865851)
XLA Ops:
  0.0 101.0 %shard_map.73 = bf16[832,384]{1,0:T(8,128)(2,1)} custom-call(bf16[832,1024]{1,0:T(8,128)(2,1)} %x_ref.1, bf16[832]{0:T(1024)(128)(2,1)} %gain_ref.1, bf16[832]{0:T(1024)(128)(2,1)} %bias_ref.1, bf16[832]{0:T(1024)(128)(2,1)} %mbias_ref.1, bf16[4,104,832]{2,1,0:T(8,128)(2,1)} %bitcast.2, s32[1,256]{1,0:T(1,128)} %bitcast.3, bf16[832,384]{1,0:T(8,128)(2,1)} %text_ref.1), custom_call_target="tpu_custom_call" | custom-call | tf_op jit(solution)/shard_map/pallas_call | solution.py:595
  101.0 2.0 %copy.9 = bf16[832,384]{1,0:T(8,128)(2,1)} copy(bf16[832,384]{1,0:T(8,128)(2,1)} %shard_map.73) | data formatting | bytes 1277952

commit v8 on v7

--- a/solution.py
+++ b/solution.py
@@ -461,15 +461,22 @@
         def _():
             token_copy(i, i, i).wait_recv()
 
+    between = (plane > 0) & (plane + 1 < planes)
+
     @pl.loop(0, planes)
     def _(far):
         for c in range(nchunks):
-            @pl.when(far > 1)
+            @pl.when((far > 1) & jnp.logical_not(between))
             def _():
                 for move in (2,) if c else (0, 1):
                     take_and_pass(far, move)
             both_sides(far, lambda zz: use_chunk(zz, c))
             owned_sides(far, c, join_chunk)
+
+            @pl.when((far > 0) & (far + 1 < planes) & between)
+            def _():
+                for move in (2,) if c else (0, 1):
+                    take_and_pass(far + 1, move)
             if c:
                 owned_sides(far, c - 1, place_chunk)
             else:

time: 103 us -> 94.9 us (0.921)
  Pallas kernels: 101 us -> 92.7 us
    pallas_call x1, Pallas kernels: 101 us -> 92.7 us  [shards(): pl.pallas_call(functools.partial(merge_kernel, nseq, ntp, slots, len(piec...]
where the time goes in v8:
time: 94.9 us; the launch traced here: 94.7 us
  Pallas kernels  92.7 us (98%)
  local copies, waits for them, and re-layouts  1.98 us (2%)
    pallas_call x1, Pallas kernels, shards(): pl.pallas_call(functools.partial(merge_kernel, nseq, ntp, slots, len(piec...  92.7 us
    unnamed x1, local copies, waits for them, and re-layouts  1.98 us

profile of v8, /device:TPU:0, one launch (start us, length us, event | category | flops | bytes accessed | tf_op | source)
XLA Modules:
  0.0 94.7 jit_solution(8410584010835224996)
XLA Ops:
  0.0 92.7 %shard_map.73 = bf16[832,384]{1,0:T(8,128)(2,1)} custom-call(bf16[832,1024]{1,0:T(8,128)(2,1)} %x_ref.1, bf16[832]{0:T(1024)(128)(2,1)} %gain_ref.1, bf16[832]{0:T(1024)(128)(2,1)} %bias_ref.1, bf16[832]{0:T(1024)(128)(2,1)} %mbias_ref.1, bf16[4,104,832]{2,1,0:T(8,128)(2,1)} %bitcast.2, s32[1,256]{1,0:T(1,128)} %bitcast.3, bf16[832,384]{1,0:T(8,128)(2,1)} %text_ref.1), custom_call_target="tpu_custom_call" | custom-call | tf_op jit(solution)/shard_map/pallas_call | solution.py:602
  92.7 2.0 %copy.9 = bf16[832,384]{1,0:T(8,128)(2,1)} copy(bf16[832,384]{1,0:T(8,128)(2,1)} %shard_map.73) | data formatting | bytes 1277952
